TPU v7x, 32 devices: a whole 2x2x4 slice. The times are simulated.
32 devices in a mesh: ctx: 4 (over y, x), ch: 8 (over z, core).
Axes of the slice: x: 2, y: 2, z: 4, core: 2. Of those that a mesh axis runs over, the one named last changes fastest.
Arguments:
- features: bfloat16 [3, 512, 8192], P(None, 'ctx', 'ch'), may hold values from -6 to 6
- short_kernel: float32 [3, 7, 8192], P(None, None, 'ch'), may hold values from -2 to 2
- long_filter: bfloat16 [512, 8192], P('ctx', 'ch'), may hold values from -0.25 to 0.25
- out_weight: bfloat16 [8192, 8192], P(None, 'ch'), may hold values from -0.0625 to 0.0625
- grad_out: bfloat16 [512, 8192], P('ctx', 'ch'), may hold values from -6 to 6
Outputs:
- grad_features: bfloat16 [3, 512, 8192], P(None, 'ctx', 'ch')
- grad_kernel: float32 [3, 7, 8192], P(None, None, 'ch')
- grad_filter: float32 [512, 8192], P('ctx', 'ch')
- grad_weight: float32 [8192, 8192], P('ctx', 'ch')
All inputs are finite; a program needn't handle non-finite values.
Results may differ from a plain program's by a relative error of at most 0.0051.
Values may be sent and summed in bfloat16 or wider, within the bound.
A program may use at most 128 MiB of HBM per device.

v0:
```python
import math

import jax
import jax.numpy as jnp
from jax import lax
from jax.sharding import PartitionSpec as P

TRIPLE = lax.Precision.HIGH


def shifted(array, axis, by):
    peers = lax.axis_size(axis)
    pairs = [(i, i + by) for i in range(peers) if 0 <= i + by < peers]
    return lax.ppermute(array, axis, pairs)


def tables(period):
    index_row = lax.iota(jnp.int32, period)
    product = index_row[:, None] * index_row[None, :] % period
    angles = product.astype(jnp.float32) * (2.0 * math.pi / period)
    return (jnp.cos(angles), jnp.sin(angles))


def spectrum(cos_part, sin_part, block):
    values = block.astype(jnp.float32)
    real_part = jnp.dot(cos_part, values, precision=TRIPLE, preferred_element_type=jnp.float32)
    imag_part = -jnp.dot(sin_part, values, precision=TRIPLE, preferred_element_type=jnp.float32)
    return (real_part, imag_part)


def inverse(cos_part, sin_part, real_part, imag_part, period):
    first = jnp.dot(cos_part, real_part, precision=TRIPLE, preferred_element_type=jnp.float32)
    second = jnp.dot(sin_part, imag_part, precision=TRIPLE, preferred_element_type=jnp.float32)
    return (first - second) / period


def pick_lag(lag_real, lag_imag, lag_index):
    lag_index = jnp.asarray(lag_index, jnp.int32)
    active = (lag_index >= 0).astype(jnp.float32)
    clipped = jnp.maximum(lag_index, 0)
    real_part = lax.dynamic_index_in_dim(lag_real, clipped, 0, keepdims=False)
    imag_part = lax.dynamic_index_in_dim(lag_imag, clipped, 0, keepdims=False)
    return (real_part, imag_part, active, clipped)


def local(features, short_kernel, long_filter, out_weight, grad_out):
    block_len = features.shape[1]
    chans = features.shape[2]
    taps = short_kernel.shape[1]
    margin = taps - 1
    blocks = lax.axis_size("ctx")
    position = lax.axis_index("ctx")
    period = 2 * block_len
    cos_table, sin_table = tables(period)
    cos_low, sin_low = (cos_table[:, :block_len], sin_table[:, :block_len])
    cos_mid, sin_mid = (
        cos_table[:, block_len - 1 : period - 1],
        sin_table[:, block_len - 1 : period - 1],
    )
    before = shifted(features[:, block_len - margin :, :], "ctx", 1)
    extended = jnp.concatenate([before, features], axis=1).astype(jnp.float32)
    conv = jnp.zeros((3, block_len, chans), jnp.float32)
    for tap_index in range(taps):
        conv = (
            conv
            + short_kernel[:, tap_index, None, :]
            * extended[:, margin - tap_index : margin - tap_index + block_len, :]
        )
    q_conv, k_conv, v_conv = (conv[0], conv[1], conv[2])
    gated = (k_conv * v_conv).astype(jnp.bfloat16)
    whole_filter = lax.all_gather(long_filter, "ctx", axis=0, tiled=True).astype(jnp.float32)
    padded = jnp.concatenate(
        [
            jnp.zeros((block_len - 1, chans), jnp.float32),
            whole_filter,
            jnp.zeros((block_len + 1, chans), jnp.float32),
        ],
        axis=0,
    )
    padded = padded.reshape(blocks + 2, block_len, chans)
    lag_time = jnp.concatenate([padded[:blocks], padded[1 : blocks + 1]], axis=1)
    lag_real = jnp.einsum(
        "fn,mnc->mfc", cos_table, lag_time, precision=TRIPLE, preferred_element_type=jnp.float32
    )
    lag_imag = -jnp.einsum(
        "fn,mnc->mfc", sin_table, lag_time, precision=TRIPLE, preferred_element_type=jnp.float32
    )
    empty = jnp.zeros((period, chans), jnp.float32)
    totals = (empty, empty)
    pieces = lax.all_gather(gated, "ctx", axis=0, tiled=True)
    first = jnp.int32(0)
    for inner in range(pieces.shape[0] // block_len):
        lag_index = position - (first // block_len + inner)
        gated_real, gated_imag = spectrum(
            cos_low, sin_low, pieces[inner * block_len : (inner + 1) * block_len]
        )
        add_filt_real, add_filt_imag, add_active, add_clipped = pick_lag(
            lag_real, lag_imag, lag_index
        )
        totals = (
            totals[0] + add_active * (add_filt_real * gated_real - add_filt_imag * gated_imag),
            totals[1] + add_active * (add_filt_real * gated_imag + add_filt_imag * gated_real),
        )
    long_out = inverse(
        cos_table[block_len - 1 : period - 1],
        sin_table[block_len - 1 : period - 1],
        totals[0],
        totals[1],
        period,
    )
    mixed = (q_conv * long_out).astype(jnp.bfloat16)
    partial_mixed = jnp.einsum(
        "tc,dc->td", grad_out, out_weight, preferred_element_type=jnp.float32
    )
    grad_mixed = lax.psum_scatter(partial_mixed, "ch", scatter_dimension=1, tiled=True)
    grad_long = (grad_mixed * q_conv).astype(jnp.bfloat16)
    own_real, own_imag = spectrum(cos_low, sin_low, gated)
    lag_empty = jnp.zeros((blocks, period, chans), jnp.float32)
    start_carry = (empty, empty, lag_empty, lag_empty)
    carry = start_carry
    pieces = lax.all_gather(grad_long, "ctx", axis=0, tiled=True)
    first = jnp.int32(0)
    for inner in range(pieces.shape[0] // block_len):
        lag_index = first // block_len + inner - position
        grad_real, grad_imag = spectrum(
            cos_mid, sin_mid, pieces[inner * block_len : (inner + 1) * block_len]
        )
        filt_real, filt_imag, active, clipped = pick_lag(lag_real, lag_imag, lag_index)
        back_real = carry[0] + active * (filt_real * grad_real + filt_imag * grad_imag)
        back_imag = carry[1] + active * (filt_real * grad_imag - filt_imag * grad_real)
        pair_real = active * (own_real * grad_real + own_imag * grad_imag)
        pair_imag = active * (own_real * grad_imag - own_imag * grad_real)
        old_real = lax.dynamic_index_in_dim(carry[2], clipped, 0, keepdims=False)
        old_imag = lax.dynamic_index_in_dim(carry[3], clipped, 0, keepdims=False)
        lags_real = lax.dynamic_update_index_in_dim(carry[2], old_real + pair_real, clipped, 0)
        lags_imag = lax.dynamic_update_index_in_dim(carry[3], old_imag + pair_imag, clipped, 0)
        carry = (back_real, back_imag, lags_real, lags_imag)
    grad_gated = inverse(cos_table[:block_len], sin_table[:block_len], carry[0], carry[1], period)
    lag_grads = (
        jnp.einsum(
            "nf,mfc->mnc", cos_table, carry[2], precision=TRIPLE, preferred_element_type=jnp.float32
        )
        - jnp.einsum(
            "nf,mfc->mnc", sin_table, carry[3], precision=TRIPLE, preferred_element_type=jnp.float32
        )
    ) / period
    upper_part = lag_grads[:, block_len - 1 : period - 1]
    lower_next = jnp.concatenate(
        [lag_grads[1:, : block_len - 1], jnp.zeros((1, block_len - 1, chans), jnp.float32)], axis=0
    )
    lower_next = jnp.concatenate([jnp.zeros((blocks, 1, chans), jnp.float32), lower_next], axis=1)
    filter_terms = (upper_part + lower_next).reshape(blocks * block_len, chans)
    grad_filter = lax.psum_scatter(filter_terms, "ctx", scatter_dimension=0, tiled=True)
    grad_conv = jnp.stack([grad_mixed * long_out, grad_gated * v_conv, grad_gated * k_conv], axis=0)
    after = shifted(grad_conv[:, :margin, :], "ctx", -1)
    grad_extended = jnp.concatenate([grad_conv, after], axis=1)
    feature_total = jnp.zeros((3, block_len, chans), jnp.float32)
    kernel_rows = []
    for tap_index in range(taps):
        feature_total = (
            feature_total
            + short_kernel[:, tap_index, None, :]
            * grad_extended[:, tap_index : tap_index + block_len, :]
        )
        kernel_rows.append(
            jnp.sum(
                grad_conv * extended[:, margin - tap_index : margin - tap_index + block_len, :],
                axis=1,
            )
        )
    grad_features = feature_total.astype(jnp.bfloat16)
    grad_kernel = lax.psum(jnp.stack(kernel_rows, axis=1), "ctx")
    weight_terms = jnp.einsum(
        "tn,tc->nc",
        lax.all_gather(mixed, "ch", axis=1, tiled=True),
        grad_out,
        preferred_element_type=jnp.float32,
    )
    grad_weight = lax.psum_scatter(weight_terms, "ctx", scatter_dimension=0, tiled=True)
    return (grad_features, grad_kernel, grad_filter, grad_weight)


def solution(mesh):
    return jax.shard_map(
        local,
        mesh=mesh,
        in_specs=(
            P(None, "ctx", "ch"),
            P(None, None, "ch"),
            P("ctx", "ch"),
            P(None, "ch"),
            P("ctx", "ch"),
        ),
        out_specs=(P(None, "ctx", "ch"), P(None, None, "ch"), P("ctx", "ch"), P("ctx", "ch")),
        check_vma=False,
    )
```

profile of v0, /device:TPU:7, one launch (start us, length us, event | category | flops | bytes accessed | tf_op | source)
XLA Modules:
  0.0 613.3 jit_solution(9139523341000812085)
XLA Ops:
  19.1 13.5 %fusion.236 = f32[128,8192]{1,0:T(8,128)} fusion(bf16[128,1024]{1,0:T(8,128)(2,1)S(1)} %copy-done, bf16[8192,1024]{1,0:T(8,128)(2,1)} %param.8), kind=kOutput, calls=%fused_computation.316 | convolution fusion | flops 2147483648 | bytes 21233664 | tf_op jit(solution)/shard_map/tc,dc->td/dot_general | solution.py:112
  34.7 2.9 all-gather.5.cloned.1.call-done
  39.1 2.6 pad_slice_fusion.1
  41.6 3.0 copy.72
  44.6 3.2 copy.73
  47.8 7.4 %fusion.2 = f32[4,1024,256]{2,1,0:T(8,128)} fusion(f32[4,128,1024]{1,2,0:T(8,128)} %copy.73, f32[4,128,1024]{1,2,0:T(8,128)} %copy.72), kind=kOutput, calls=%fused_computation.6 | convolution fusion | flops 1613627392 | bytes 8388608 | tf_op jit(solution)/shard_map/fn,mnc->mfc/dot_general | solution.py:85
  55.2 4.8 fusion.1
  60.0 6.7 %all-gather.7.cloned.1.call-done = bf16[512,1024]{1,0:T(8,128)(2,1)} async-done(((bf16[128,1024]{1,0:T(8,128)(2,1)}), bf16[512,1024]{1,0:T(8,128)(2,1)}) %all-gather.7.cloned.1.call-update) | async-done | bytes 1048592 | tf_op jit(solution)/shard_map/all_gather | solution.py:90
  78.2 4.8 reduce-scatter.4.cloned.1.call-done
  83.0 8.8 %multiply_convert_fusion = (bf16[128,1024]{1,0:T(8,128)(2,1)}, bf16[128,1024]{1,0:T(8,128)(2,1)}, f32[1,128,1024]{2,1,0:T(8,128)}) fusion(f32[3,128,1024]{2,1,0:T(8,128)} %copy-done.38, f32[128,1024]{1,0:T(8,128)} %reduce-scatter.4.cloned.1.call-done, f32[128,1024]{1,0:T(8,128)} %fusion.52, f32[256,1024]{0,1:T(8,128)} %copy-done.34, ...), kind=kOutput, calls=%fused_computation.175 | convolution fusion | flops 207224832 | bytes 19529760 | tf_op jit(solution)/shard_map/dot_general | solution.py:33
  95.8 21.8 %all-gather.9.cloned.1.call-done = bf16[512,1024]{1,0:T(8,128)(2,1)} async-done(((bf16[128,1024]{1,0:T(8,128)(2,1)}), bf16[512,1024]{1,0:T(8,128)(2,1)}) %all-gather.9.cloned.1.call-update) | async-done | bytes 1048592 | tf_op jit(solution)/shard_map/all_gather | solution.py:121
  122.7 2.5 copy.124
  139.2 2.6 copy.125
  145.1 3.4 fusion.14
  155.7 2.5 copy.129
  165.4 2.6 copy.109
  171.4 3.4 fusion.13
  174.8 2.6 copy.132
  182.1 2.6 copy.133
  184.7 2.6 copy.114
  191.9 2.6 copy.115
  197.9 3.4 fusion.12
  201.3 2.7 copy.136
  209.9 6.3 %fusion.141 = f32[4,1024,256]{1,2,0:T(8,128)S(1)} fusion(f32[4,256,1024]{2,1,0:T(8,128)} %constant_dynamic-update-slice_fusion.12), kind=kOutput, calls=%fused_computation.205 | convolution fusion | flops 1611530240 | bytes 8388608 | tf_op jit(solution)/shard_map/nf,mfc->mnc/dot_general | solution.py:140
  216.4 4.3 multiply_bitcast_fusion
  226.2 2.8 multiply_bitcast_fusion.4
  232.2 4.1 pad_add_fusion
  236.6 14.8 %fusion.237 = f32[8192,1024]{1,0:T(8,128)} fusion(bf16[128,8192]{1,0:T(8,128)(2,1)} %all-gather.11.cloned.1.call-done, bf16[128,1024]{1,0:T(8,128)(2,1)S(1)} %copy-done), kind=kOutput, calls=%fused_computation.317 | convolution fusion | flops 2147483648 | bytes 35913728 | tf_op jit(solution)/shard_map/tn,tc->nc/dot_general | solution.py:173
  252.5 3.1 collective-permute-start.1
  259.5 14.5 %all-reduce.6.cloned.1.call-done = f32[3,7,1024]{2,0,1:T(4,128)} async-done(((f32[3,7,1024]{2,0,1:T(4,128)}), f32[3,7,1024]{2,0,1:T(4,128)}) %all-reduce.6.cloned.1.call-update) | async-done | bytes 86032 | tf_op jit(solution)/shard_map/psum | solution.py:172
  275.6 37.7 %reduce-scatter.6.cloned.1.call-done = f32[128,1024]{1,0:T(8,128)} async-done(((f32[512,1024]{1,0:T(8,128)}), f32[128,1024]{1,0:T(8,128)}) %reduce-scatter.6.cloned.1.call-update) | async-done | bytes 524304 | tf_op jit(solution)/shard_map/reduce_scatter | solution.py:153
  313.3 292.3 %reduce-scatter.8.cloned.1.call-done = f32[2048,1024]{1,0:T(8,128)} async-done(((f32[8192,1024]{1,0:T(8,128)}), f32[2048,1024]{1,0:T(8,128)}) %reduce-scatter.8.cloned.1.call-update) | async-done | bytes 8388624 | tf_op jit(solution)/shard_map/reduce_scatter | solution.py:179
  (203 shorter events, 103.4 us)
Async XLA Ops:
  8.0 11.1 %copy-start = (bf16[128,1024]{1,0:T(8,128)(2,1)S(1)}, bf16[128,1024]{1,0:T(8,128)(2,1)}, u32[]{:S(2)}) copy-start(bf16[128,1024]{1,0:T(8,128)(2,1)} %param.9) | copy-start | bytes 786436
  8.0 29.6 %all-gather.5.cloned.1.call-start = ((), (), s32[]{:S(2)}) async-start(), calls=%async_computation.4 | async-start | bytes 1310720 | tf_op jit(solution)/shard_map/all_gather | solution.py:71
  8.7 57.9 %all-gather.7.cloned.1.call-start = ((), (), s32[]{:S(2)}) async-start(), calls=%async_computation.5 | async-start | bytes 1310720 | tf_op jit(solution)/shard_map/all_gather | solution.py:90
  9.6 4.8 collective-permute-start
  12.3 4.8 copy-start.50
  19.1 63.9 %reduce-scatter.4.cloned.1.call-start = ((), (), s32[]{:S(2)}) async-start(), calls=%async_computation.3 | async-start | bytes 4718592 | tf_op jit(solution)/shard_map/reduce_scatter | solution.py:115
  32.7 85.0 %all-gather.9.cloned.1.call-start = ((), (), s32[]{:S(2)}) async-start(), calls=%async_computation.6 | async-start | bytes 1310720 | tf_op jit(solution)/shard_map/all_gather | solution.py:121
  47.8 7.4 %copy-start.12 = (f32[4,128,1024]{1,2,0:T(8,128)S(1)}, f32[4,128,1024]{1,2,0:T(8,128)}, u32[]{:S(2)}) copy-start(f32[4,128,1024]{1,2,0:T(8,128)} %copy.72) | copy-start | bytes 6291460
  47.8 7.4 %copy-start.13 = (f32[4,128,1024]{1,2,0:T(8,128)S(1)}, f32[4,128,1024]{1,2,0:T(8,128)}, u32[]{:S(2)}) copy-start(f32[4,128,1024]{1,2,0:T(8,128)} %copy.73) | copy-start | bytes 6291460
  91.8 144.8 %all-gather.11.cloned.1.call-start = ((), (), s32[]{:S(2)}) async-start(), calls=%async_computation.9 | async-start | bytes 2359296 | tf_op jit(solution)/shard_map/all_gather | solution.py:175
  95.8 178.3 %all-reduce.6.cloned.1.call-start = ((), (), s32[]{:S(2)}) async-start(), calls=%async_computation.7 | async-start | bytes 229376 | tf_op jit(solution)/shard_map/psum | solution.py:172
  143.4 5.1 copy-start.18
  169.7 5.1 copy-start.22
  196.1 5.1 copy-start.26
  201.3 5.0 copy-start.45
  209.9 6.4 %copy-start.6 = (f32[4,256,1024]{2,1,0:T(8,128)S(1)}, f32[4,256,1024]{2,1,0:T(8,128)}, u32[]{:S(2)}) copy-start(f32[4,256,1024]{2,1,0:T(8,128)} %constant_dynamic-update-slice_fusion.8) | copy-start | bytes 12582916
  209.9 12.1 %copy-start.29 = (f32[256,1024]{0,1:T(8,128)S(1)}, f32[256,1024]{0,1:T(8,128)}, u32[]{:S(2)}) copy-start(f32[256,1024]{0,1:T(8,128)} %copy-done.28) | copy-start | bytes 3145732
  216.3 5.7 copy-start.2
  216.3 5.7 copy-start.4
  216.3 5.7 copy-start.21
  216.3 5.7 copy-start.23
  216.3 5.7 copy-start.25
  216.3 5.7 copy-start.27
  220.6 5.5 copy-start.30
  232.1 81.2 %reduce-scatter.6.cloned.1.call-start = ((), (), s32[]{:S(2)}) async-start(), calls=%async_computation.8 | async-start | bytes 2621440 | tf_op jit(solution)/shard_map/reduce_scatter | solution.py:153
  236.3 369.3 %reduce-scatter.8.cloned.1.call-start = ((), (), s32[]{:S(2)}) async-start(), calls=%async_computation.10 | async-start | bytes 41943040 | tf_op jit(solution)/shard_map/reduce_scatter | solution.py:179
  251.4 5.7 copy-start.41
  251.5 5.8 copy-start.51
  251.5 5.8 copy-start.53
  251.5 5.8 copy-start.55
  251.5 5.8 copy-start.57
  252.5 4.7 collective-permute-start.1
  (36 other events, 100.2 us)
Sparse Core Ops, SparseCore 0:
  10.7 26.8 all-gather.4
  40.0 26.6 all-gather.6
  91.9 25.6 all-gather.8
  119.1 30.3 all-gather.10
  232.3 41.7 all-reduce.5
  277.7 35.5 reduce-scatter.5
  316.9 288.6 reduce-scatter.7
Sparse Core Ops, SparseCore 1:
  32.7 50.2 reduce-scatter.3
where the time goes:
time: 624 us; the launch traced here: 613 us
  waiting for transfers between devices  385 us (62%)
  matrix products  89.5 us (14%)
  local copies, waits for them, and re-layouts  89.3 us (14%)
  other arithmetic  27.6 us (4%)
  between operations  16.8 us (3%)
    reduce_scatter x1, waiting for transfers between devices, local(): lax.psum_scatter(weight_terms, 'ctx', scatter_dimension=0, tiled=True)  292 us
    reduce_scatter x1, waiting for transfers between devices, local(): lax.psum_scatter(filter_terms, 'ctx', scatter_dimension=0, tiled=True)  37.7 us
    all_gather x1, waiting for transfers between devices, local(): pieces = lax.all_gather(grad_long, 'ctx', axis=0, tiled=True)  21.8 us
    dot_general x1, matrix products, local(): jnp.einsum('tn,tc->nc', lax.all_gather(mixed, 'ch', axis=1, tiled=True),...  14.8 us
    unnamed x127, local copies, waits for them, and re-layouts  14.8 us
    psum x1, waiting for transfers between devices, local(): grad_kernel = lax.psum(jnp.stack(kernel_rows, axis=1), 'ctx')  14.5 us
    dot_general x1, matrix products, local(): jnp.einsum('tc,dc->td', grad_out, out_weight, preferred_element_type=jnp....  13.5 us
    dynamic_slice x6, local copies, waits for them, and re-layouts, local(): old_imag = lax.dynamic_index_in_dim(carry[3], clipped, 0, keepdims=False)  13.5 us
  transfers between devices with their start and end apart: 10, of which 9 were waited for; matrix products, arithmetic and copies ran while one was open for 30% of the time, Pallas kernels for 0%

commit v1 on v0

v1 whole, which is shorter than its diff:
```python
import numpy as np

import jax
import jax.numpy as jnp
from jax import lax
from jax.sharding import PartitionSpec as P

BF16 = jnp.bfloat16
F32 = jnp.float32


def fourier_tables(length):
    period = 2 * length
    freq = np.arange(length)
    angles = (freq[:, None] * np.arange(length)[None, :] % period) * (2 * np.pi / period)
    cos_part, sin_part = np.cos(angles), -np.sin(angles)
    sin_part[0] = 1 - 2 * (np.arange(length) % 2)
    ahead = np.concatenate([cos_part, sin_part], axis=0)
    weight = np.full((length, 1), 2.0 / period)
    weight[0] = 1.0 / period
    back = np.concatenate([cos_part * weight, sin_part * weight], axis=0).T

    def halves(table):
        high = table.astype(np.float32).astype(BF16)
        low = (table - high.astype(np.float64)).astype(np.float32).astype(BF16)
        return high, low

    return halves(ahead) + halves(back)


def to_spectrum(high, low, block):
    return jnp.dot(high, block, preferred_element_type=F32) + jnp.dot(
        low, block, preferred_element_type=F32
    )


def from_spectrum(high, low, real_part, imag_part):
    half = real_part.shape[0]
    total = None
    for values, columns in ((real_part, slice(0, half)), (imag_part, slice(half, 2 * half))):
        upper = values.astype(BF16)
        rest = (values - upper.astype(F32)).astype(BF16)
        term = (
            jnp.dot(high[:, columns], upper, preferred_element_type=F32)
            + jnp.dot(low[:, columns], upper, preferred_element_type=F32)
            + jnp.dot(high[:, columns], rest, preferred_element_type=F32)
        )
        total = term if total is None else total + term
    return total


def spectral_product(first, second, conjugate):
    half = first.shape[0] // 2
    first_real, first_imag = first[:half], first[half:]
    second_real, second_imag = second[:half], second[half:]
    edge = lax.broadcasted_iota(jnp.int32, first_real.shape, 0) == 0
    real_real = first_real * second_real
    imag_imag = first_imag * second_imag
    if conjugate:
        real_part = real_real + imag_imag
        imag_part = first_real * second_imag - first_imag * second_real
    else:
        real_part = real_real - imag_imag
        imag_part = first_real * second_imag + first_imag * second_real
    return jnp.where(edge, real_real, real_part), jnp.where(edge, imag_imag, imag_part)


def shifted(array, axis, by):
    peers = lax.axis_size(axis)
    pairs = [(i, i + by) for i in range(peers) if 0 <= i + by < peers]
    return lax.ppermute(array, axis, pairs)


def whole_sequence(block):
    return lax.all_to_all(block, "ctx", split_axis=1, concat_axis=0, tiled=True)


def own_tokens(block):
    return lax.all_to_all(block, "ctx", split_axis=0, concat_axis=1, tiled=True)


def plain(features, short_kernel, long_filter, out_weight, grad_out):
    block_len, chans = features.shape[1:]
    taps = short_kernel.shape[1]
    margin = taps - 1
    ahead_high, ahead_low, back_high, back_low = fourier_tables(block_len * lax.axis_size("ctx"))
    partial_mixed = jnp.einsum("tc,dc->td", grad_out, out_weight, preferred_element_type=F32)
    grad_mixed = lax.psum_scatter(partial_mixed, "ch", scatter_dimension=1, tiled=True)
    before = shifted(features[:, block_len - margin :, :], "ctx", 1)
    extended = jnp.concatenate([before, features], axis=1).astype(F32)
    conv = jnp.zeros((3, block_len, chans), F32)
    for tap_index in range(taps):
        conv = (
            conv
            + short_kernel[:, tap_index, None, :]
            * extended[:, margin - tap_index : margin - tap_index + block_len, :]
        )
    q_conv, k_conv, v_conv = (conv[0], conv[1], conv[2])
    gated = (k_conv * v_conv).astype(BF16)
    filter_spec = to_spectrum(ahead_high, ahead_low, whole_sequence(long_filter))
    gated_spec = to_spectrum(ahead_high, ahead_low, whole_sequence(gated))
    out_spec = spectral_product(filter_spec, gated_spec, False)
    long_out = own_tokens(from_spectrum(back_high, back_low, *out_spec))
    mixed = (q_conv * long_out).astype(BF16)
    grad_long = (grad_mixed * q_conv).astype(BF16)
    grad_spec = to_spectrum(ahead_high, ahead_low, whole_sequence(grad_long))
    back_spec = spectral_product(filter_spec, grad_spec, True)
    grad_gated = own_tokens(from_spectrum(back_high, back_low, *back_spec))
    lag_spec = spectral_product(gated_spec, grad_spec, True)
    grad_filter = own_tokens(from_spectrum(back_high, back_low, *lag_spec))
    grad_conv = jnp.stack([grad_mixed * long_out, grad_gated * v_conv, grad_gated * k_conv], axis=0)
    after = shifted(grad_conv[:, :margin, :], "ctx", -1)
    grad_extended = jnp.concatenate([grad_conv, after], axis=1)
    feature_total = jnp.zeros((3, block_len, chans), F32)
    kernel_rows = []
    for tap_index in range(taps):
        feature_total = (
            feature_total
            + short_kernel[:, tap_index, None, :]
            * grad_extended[:, tap_index : tap_index + block_len, :]
        )
        kernel_rows.append(
            jnp.sum(
                grad_conv * extended[:, margin - tap_index : margin - tap_index + block_len, :],
                axis=1,
            )
        )
    grad_features = feature_total.astype(BF16)
    grad_kernel = lax.psum(jnp.stack(kernel_rows, axis=1), "ctx")
    all_mixed = whole_sequence(lax.all_gather(mixed, "ch", axis=1, tiled=True))
    all_grad_out = lax.all_gather(grad_out, "ctx", axis=0, tiled=True)
    grad_weight = jnp.einsum("tn,tc->nc", all_mixed, all_grad_out, preferred_element_type=F32)
    return (grad_features, grad_kernel, grad_filter, grad_weight)


def solution(mesh):
    return jax.shard_map(
        plain,
        mesh=mesh,
        in_specs=(
            P(None, "ctx", "ch"),
            P(None, None, "ch"),
            P("ctx", "ch"),
            P(None, "ch"),
            P("ctx", "ch"),
        ),
        out_specs=(P(None, "ctx", "ch"), P(None, None, "ch"), P("ctx", "ch"), P("ctx", "ch")),
        check_vma=False,
    )
```

time: 624 us -> 221 us (0.35); the launches traced: 613 us -> 217 us
  waiting for transfers between devices: 385 us -> 86.9 us
  local copies, waits for them, and re-layouts: 89.3 us -> 29.4 us
  matrix products: 89.5 us -> 35.1 us
  starting transfers between devices: 4.91 us -> 32.2 us
  other arithmetic: 27.6 us -> 10.7 us
  blocking collectives: 0 us -> 8.29 us
    reduce_scatter x3 -> x1, waiting for transfers between devices: 335 us -> 10.8 us  [plain(): lax.psum_scatter(partial_mixed, 'ch', scatter_dimension=1, tiled=True)]
    dot_general x28 -> x26, matrix products: 89.5 us -> 35.1 us  [the longest x1 13.4 us: plain(): jnp.einsum('tc,dc->td', grad_out, out_weight, preferred_element_type=F32)]
    all_to_all x0 -> x6, starting transfers between devices: none -> 28.3 us  [the longest x4 17.3 us: whole_sequence(): return lax.all_to_all(block, 'ctx', split_axis=1, concat_axis=0, tiled=True)]
    dynamic_slice x12 -> x0, local copies, waits for them, and re-layouts: 26.9 us -> none  [the longest x6 13.5 us: local(): old_imag = lax.dynamic_index_in_dim(carry[3], clipped, 0, keepdims=False)]
    broadcast_in_dim x10 -> x0, local copies, waits for them, and re-layouts: 20.3 us -> none  [the longest x4 10.4 us: local(): lax.dynamic_update_index_in_dim(carry[3], old_imag + pair_imag, clipped, 0)]
    all_to_all x0 -> x12, local copies, waits for them, and re-layouts: none -> 14.3 us  [the longest x6 8.2 us: own_tokens(): return lax.all_to_all(block, 'ctx', split_axis=0, concat_axis=1, tiled=True)]
    dynamic_update_slice x8 -> x0, local copies, waits for them, and re-layouts: 14.1 us -> none  [the longest x4 7.04 us: local(): lax.dynamic_update_index_in_dim(carry[3], old_imag + pair_imag, clipped, 0)]
    ppermute x2, waiting for transfers between devices: 3.71 us -> 17.1 us  [shifted(): return lax.ppermute(array, axis, pairs)]
  transfers between devices with their start and end apart: 10 -> 12, of which waited for: 9 -> 6; matrix products, arithmetic and copies ran while one was open for 30% -> 18% of each run, Pallas kernels for 0% -> 0%
where the time goes in v1:
time: 221 us; the launch traced here: 217 us
  waiting for transfers between devices  86.9 us (39%)
  matrix products  35.1 us (16%)
  starting transfers between devices  32.2 us (15%)
  local copies, waits for them, and re-layouts  29.4 us (13%)
  between operations  14.4 us (7%)
  other arithmetic  10.7 us (5%)
  blocking collectives  8.29 us (4%)
    psum x1, waiting for transfers between devices, plain(): grad_kernel = lax.psum(jnp.stack(kernel_rows, axis=1), 'ctx')  27.5 us
    all_gather x1, waiting for transfers between devices, plain(): all_grad_out = lax.all_gather(grad_out, 'ctx', axis=0, tiled=True)  27.3 us
    all_to_all x4, starting transfers between devices, whole_sequence(): return lax.all_to_all(block, 'ctx', split_axis=1, concat_axis=0, tiled=True)  17.3 us
    ppermute x2, waiting for transfers between devices, shifted(): return lax.ppermute(array, axis, pairs)  17.1 us
    dot_general x1, matrix products, plain(): jnp.einsum('tc,dc->td', grad_out, out_weight, preferred_element_type=F32)  13.4 us
    unnamed x91, local copies, waits for them, and re-layouts  12.9 us
    all_to_all x2, starting transfers between devices, own_tokens(): return lax.all_to_all(block, 'ctx', split_axis=0, concat_axis=1, tiled=True)  11 us
    reduce_scatter x1, waiting for transfers between devices, plain(): lax.psum_scatter(partial_mixed, 'ch', scatter_dimension=1, tiled=True)  10.8 us
  transfers between devices with their start and end apart: 12, of which 6 were waited for; matrix products, arithmetic and copies ran while one was open for 18% of the time, Pallas kernels for 0%

profile of v1, /device:TPU:7, one launch (start us, length us, event | category | flops | bytes accessed | tf_op | source)
XLA Modules:
  0.0 216.9 jit_solution(18053277490159083799)
XLA Ops:
  7.2 13.4 %fusion.40 = f32[128,8192]{1,0:T(8,128)} fusion(bf16[128,1024]{1,0:T(8,128)(2,1)} %param.29, bf16[8192,1024]{1,0:T(8,128)(2,1)} %param.28), kind=kOutput, calls=%fused_computation.112 | convolution fusion | flops 2147483648 | bytes 21233664 | tf_op jit(solution)/shard_map/tc,dc->td/dot_general | solution.py:87
  21.8 1.4 collective-permute-start
  24.3 5.4 %all-to-all-start = ((bf16[128,4,256]{2,0,1:T(8,128)(2,1)}), bf16[128,4,256]{2,0,1:T(8,128)(2,1)S(1)}, u32[]{:S(2)}, u32[]{:S(2)}) async-start(bf16[128,4,256]{2,0,1:T(8,128)(2,1)} %copy.60), calls=%async_computation.1 | async-start | bytes 524288 | tf_op jit(solution)/shard_map/all_to_all | solution.py:75
  30.6 1.3 multiply_add_fusion
  34.1 3.6 %all-to-all-start.1 = ((bf16[128,4,256]{2,0,1:T(8,128)(2,1)}), bf16[128,4,256]{2,0,1:T(8,128)(2,1)S(1)}, u32[]{:S(2)}, u32[]{:S(2)}) async-start(bf16[128,4,256]{2,0,1:T(8,128)(2,1)} %copy.62), calls=%async_computation.2 | async-start | bytes 524288 | tf_op jit(solution)/shard_map/all_to_all | solution.py:75
  40.9 1.4 convolution_add_fusion.2
  50.7 8.3 %all_to_all.130 = f32[4,128,256]{2,1,0:T(8,128)S(1)} all-to-all(f32[4,128,256]{2,1,0:T(8,128)} %bitcast.111), channel_id=1, replica_groups=mesh['ctx'=4,'ch'=8] {'ctx'}, dimensions={0} | all-to-all | bytes 1048576 | tf_op jit(solution)/shard_map/all_to_all | solution.py:79
  59.0 10.8 %reduce-scatter.2.cloned.1.call-done = f32[128,1024]{1,0:T(8,128)} async-done(((f32[128,8192]{1,0:T(8,128)}), f32[128,1024]{1,0:T(8,128)}) %reduce-scatter.2.cloned.1.call-update) | async-done | bytes 524304 | tf_op jit(solution)/shard_map/reduce_scatter | solution.py:88
  69.9 2.2 %multiply_convert_fusion = (bf16[128,1024]{1,0:T(8,128)(2,1)}, bf16[128,1024]{1,0:T(8,128)(2,1)S(1)}, f32[1,128,1024]{2,1,0:T(8,128)}) fusion(f32[128,1024]{1,0:T(8,128)S(1)} %bitcast.107, f32[3,128,1024]{2,1,0:T(8,128)} %copy-done.2, f32[128,1024]{1,0:T(8,128)} %reduce-scatter.2.cloned.1.call-done), kind=kLoop, calls=%fused_computation.53 | loop fusion | flops 655360 | bytes 2621440 | tf_op jit(solution)/shard_map/convert_element_type | solution.py:104
  72.8 3.7 %all-to-all-start.3 = ((bf16[128,4,256]{2,0,1:T(8,128)(2,1)}), bf16[128,4,256]{2,0,1:T(8,128)(2,1)S(1)}, u32[]{:S(2)}, u32[]{:S(2)}) async-start(bf16[128,4,256]{2,0,1:T(8,128)(2,1)} %bitcast.104), calls=%async_computation.4 | async-start | bytes 524288 | tf_op jit(solution)/shard_map/all_to_all | solution.py:75
  77.2 2.1 all-to-all-done.3
  79.6 1.7 fusion.44
  82.9 1.2 subtract_select_fusion.1
  84.0 1.2 fusion.17
  88.5 2.0 copy.83
  90.5 5.5 %all-to-all-start.4 = ((f32[4,128,256]{2,1,0:T(8,128)}), f32[4,128,256]{2,1,0:T(8,128)}, u32[]{:S(2)}, u32[]{:S(2)}) async-start(f32[4,128,256]{2,1,0:T(8,128)} %bitcast.110), calls=%async_computation.5 | async-start | bytes 1048576 | tf_op jit(solution)/shard_map/all_to_all | solution.py:79
  96.1 1.5 fusion.21
  100.7 5.5 %all-to-all-start.5 = ((f32[4,128,256]{1,2,0:T(8,128)}), f32[4,128,256]{1,2,0:T(8,128)}, u32[]{:S(2)}, u32[]{:S(2)}) async-start(f32[4,128,256]{1,2,0:T(8,128)} %bitcast.109), calls=%async_computation.6 | async-start | bytes 1048576 | tf_op jit(solution)/shard_map/all_to_all | solution.py:79
  106.2 2.2 %copy.73 = f32[128,4,256]{2,1,0:T(4,128)} copy(f32[128,4,256]{2,0,1:T(8,128)} %bitcast.10) | data formatting | bytes 1048576 | tf_op jit(solution)/shard_map/all_to_all | solution.py:79
  108.4 2.1 all_to_all.114
  110.5 1.2 slice_multiply_fusion.6
  111.7 1.6 multiply_reduce_fusion
  114.7 3.2 %copy.105 = bf16[16,4,8,2048]{3,2,0,1:T(8,128)(2,1)} copy(bf16[16,4,8,2048]{3,2,1,0:T(8,128)(2,1)} %bitcast.108) | data formatting | bytes 4194304 | tf_op jit(solution)/shard_map/all_to_all | solution.py:75
  117.8 4.6 %all-to-all-start.6 = ((bf16[128,4,2048]{2,0,1:T(8,128)(2,1)}), bf16[128,4,2048]{2,0,1:T(8,128)(2,1)}, u32[]{:S(2)}, u32[]{:S(2)}) async-start(bf16[128,4,2048]{2,0,1:T(8,128)(2,1)} %bitcast.106), calls=%async_computation.7 | async-start | bytes 4194304 | tf_op jit(solution)/shard_map/all_to_all | solution.py:75
  122.5 2.3 %collective-permute-start.1 = (f32[3,6,1024]{2,1,0:T(8,128)S(1)}, f32[3,6,1024]{2,1,0:T(8,128)S(1)}, u32[]{:S(2)}, u32[]{:S(2)}) collective-permute-start(f32[3,6,1024]{2,1,0:T(8,128)S(1)} %slice.160), channel_id=1, source_target_pairs={{8,0},{16,8},{24,16},{9,1},{17,9},{25,17},{10,2},{18,10},{26,18},{... | collective-permute-start | bytes 221192 | tf_op jit(solution)/shard_map/ppermute | solution.py:71
  124.8 2.0 copy.77
  126.9 17.1 %collective-permute-done.1 = f32[3,6,1024]{2,1,0:T(8,128)S(1)} collective-permute-done((f32[3,6,1024]{2,1,0:T(8,128)S(1)}, f32[3,6,1024]{2,1,0:T(8,128)S(1)}, u32[]{:S(2)}, u32[]{:S(2)}) %collective-permute-start.1) | collective-permute-done | bytes 73760 | tf_op jit(solution)/shard_map/ppermute | solution.py:71
  144.1 2.2 %fusion.1 = bf16[3,128,1024]{2,1,0:T(8,128)(2,1)} fusion(f32[3,134,1024]{2,1,0:T(8,128)S(1)} %pad_maximum_fusion, f32[3,1024]{1,0:T(4,128)S(1)} %copy-done.32, f32[3,1024]{1,0:T(4,128)S(1)} %copy-done.34, f32[3,1024]{1,0:T(4,128)S(1)} %get-tuple-element.49, f32[3,1024]{1,0:T(4,128)S(1)} %get-tuple-element.50, f32[3,1024]{1,0:T(4,128)S(1)} %get-tuple-element.51, ...), kind=kLoop, calls=%fused_computation.4 | loop fusion | flops 6291456 | bytes 11882496 | tf_op jit(solution)/shard_map/convert_element_type | solution.py:128
  146.3 27.5 %all-reduce.2.cloned.1.call-done = f32[3,7,1024]{2,0,1:T(4,128)} async-done(((f32[3,7,1024]{2,0,1:T(4,128)}), f32[3,7,1024]{2,0,1:T(4,128)}) %all-reduce.2.cloned.1.call-update) | async-done | bytes 86032 | tf_op jit(solution)/shard_map/psum | solution.py:129
  173.8 1.6 copy.76
  175.4 27.3 %all-gather.5.cloned.1.call-done = bf16[512,1024]{1,0:T(8,128)(2,1)} async-done(((bf16[128,1024]{1,0:T(8,128)(2,1)}), bf16[512,1024]{1,0:T(8,128)(2,1)}) %all-gather.5.cloned.1.call-update) | async-done | bytes 1048592 | tf_op jit(solution)/shard_map/all_gather | solution.py:131
  202.7 7.6 %fusion.42 = f32[2048,1024]{1,0:T(8,128)} fusion(bf16[512,2048]{1,0:T(8,128)(2,1)} %bitcast.22, bf16[512,1024]{1,0:T(8,128)(2,1)} %all-gather.5.cloned.1.call-done), kind=kOutput, calls=%fused_computation.114 | convolution fusion | flops 2147483648 | bytes 11534336 | tf_op jit(solution)/shard_map/tn,tc->nc/dot_general | solution.py:132
  (146 shorter events, 27.7 us)
Async XLA Ops:
  7.2 62.7 %reduce-scatter.2.cloned.1.call-start = ((), (), s32[]{:S(2)}) async-start(), calls=%async_computation.8 | async-start | bytes 4718592 | tf_op jit(solution)/shard_map/reduce_scatter | solution.py:88
  20.6 2.6 %copy-start.27 = (bf16[128,1024]{1,0:T(8,128)(2,1)S(1)}, bf16[128,1024]{1,0:T(8,128)(2,1)}, u32[]{:S(2)}) copy-start(bf16[128,1024]{1,0:T(8,128)(2,1)} %param.27) | copy-start | bytes 786436
  21.8 7.9 %copy-start.37 = (f32[3,7,1024]{2,1,0:T(8,128)S(1)}, f32[3,7,1024]{2,1,0:T(8,128)}, u32[]{:S(2)}) copy-start(f32[3,7,1024]{2,1,0:T(8,128)} %param.26) | copy-start | bytes 258052
  21.8 8.5 %collective-permute-start = (bf16[3,6,1024]{2,1,0:T(8,128)(2,1)S(1)}, bf16[3,6,1024]{2,1,0:T(8,128)(2,1)S(1)}, u32[]{:S(2)}, u32[]{:S(2)}) collective-permute-start(bf16[3,6,1024]{2,1,0:T(8,128)(2,1)S(1)} %slice.115), channel_id=1, source_target_pairs={{0,8},{8,16},{16,24},{1,9},{9,17},{17,25},{2,10},{10,18},{18,26},{... | collective-permute-start | bytes 110600 | tf_op jit(solution)/shard_map/ppermute | solution.py:71
  24.3 9.8 %all-to-all-start = ((bf16[128,4,256]{2,0,1:T(8,128)(2,1)}), bf16[128,4,256]{2,0,1:T(8,128)(2,1)S(1)}, u32[]{:S(2)}, u32[]{:S(2)}) async-start(bf16[128,4,256]{2,0,1:T(8,128)(2,1)} %copy.60), calls=%async_computation.1 | async-start | bytes 524288 | tf_op jit(solution)/shard_map/all_to_all | solution.py:75
  29.8 2.1 copy-start.29
  29.8 2.1 copy-start.31
  29.8 2.1 copy-start.33
  33.1 6.5 %copy-start.4 = (bf16[1024,512]{1,0:T(8,128)(2,1)S(1)}, bf16[1024,512]{1,0:T(8,128)(2,1)}, u32[]{:S(2)}) copy-start(bf16[1024,512]{1,0:T(8,128)(2,1)} %constant.24) | copy-start | bytes 3145732
  34.1 8.2 %all-to-all-start.1 = ((bf16[128,4,256]{2,0,1:T(8,128)(2,1)}), bf16[128,4,256]{2,0,1:T(8,128)(2,1)S(1)}, u32[]{:S(2)}, u32[]{:S(2)}) async-start(bf16[128,4,256]{2,0,1:T(8,128)(2,1)} %copy.62), calls=%async_computation.2 | async-start | bytes 524288 | tf_op jit(solution)/shard_map/all_to_all | solution.py:75
  72.8 6.5 %all-to-all-start.3 = ((bf16[128,4,256]{2,0,1:T(8,128)(2,1)}), bf16[128,4,256]{2,0,1:T(8,128)(2,1)S(1)}, u32[]{:S(2)}, u32[]{:S(2)}) async-start(bf16[128,4,256]{2,0,1:T(8,128)(2,1)} %bitcast.104), calls=%async_computation.4 | async-start | bytes 524288 | tf_op jit(solution)/shard_map/all_to_all | solution.py:75
  76.4 38.2 %all-gather.3.cloned.1.call-start = ((), (), s32[]{:S(2)}) async-start(), calls=%async_computation.10 | async-start | bytes 2359296 | tf_op jit(solution)/shard_map/all_gather | solution.py:130
  79.6 1.8 copy-start.7
  90.5 10.2 %all-to-all-start.4 = ((f32[4,128,256]{2,1,0:T(8,128)}), f32[4,128,256]{2,1,0:T(8,128)}, u32[]{:S(2)}, u32[]{:S(2)}) async-start(f32[4,128,256]{2,1,0:T(8,128)} %bitcast.110), calls=%async_computation.5 | async-start | bytes 1048576 | tf_op jit(solution)/shard_map/all_to_all | solution.py:79
  96.1 1.6 copy-start.25
  96.1 1.9 copy-start.18
  96.1 1.9 copy-start.21
  100.7 9.8 %copy-start.3 = (f32[3,128,1024]{2,1,0:T(8,128)S(1)}, f32[3,128,1024]{2,1,0:T(8,128)}, u32[]{:S(2)}) copy-start(f32[3,128,1024]{2,1,0:T(8,128)} %copy-done.2) | copy-start | bytes 4718596
  100.7 17.1 %all-to-all-start.5 = ((f32[4,128,256]{1,2,0:T(8,128)}), f32[4,128,256]{1,2,0:T(8,128)}, u32[]{:S(2)}, u32[]{:S(2)}) async-start(f32[4,128,256]{1,2,0:T(8,128)} %bitcast.109), calls=%async_computation.6 | async-start | bytes 1048576 | tf_op jit(solution)/shard_map/all_to_all | solution.py:79
  106.2 67.6 %all-reduce.2.cloned.1.call-start = ((), (), s32[]{:S(2)}) async-start(), calls=%async_computation.9 | async-start | bytes 229376 | tf_op jit(solution)/shard_map/psum | solution.py:129
  111.7 1.6 copy-start.14
  111.7 1.6 copy-start.16
  114.1 88.7 %all-gather.5.cloned.1.call-start = ((), (), s32[]{:S(2)}) async-start(), calls=%async_computation.11 | async-start | bytes 1310720 | tf_op jit(solution)/shard_map/all_gather | solution.py:131
  117.8 26.1 %copy-start.17 = (f32[1,128,1024]{2,1,0:T(8,128)S(1)}, f32[1,128,1024]{2,1,0:T(8,128)}, u32[]{:S(2)}) copy-start(f32[1,128,1024]{2,1,0:T(8,128)} %copy-done.16) | copy-start | bytes 1572868
  117.8 84.9 %all-to-all-start.6 = ((bf16[128,4,2048]{2,0,1:T(8,128)(2,1)}), bf16[128,4,2048]{2,0,1:T(8,128)(2,1)}, u32[]{:S(2)}, u32[]{:S(2)}) async-start(bf16[128,4,2048]{2,0,1:T(8,128)(2,1)} %bitcast.106), calls=%async_computation.7 | async-start | bytes 4194304 | tf_op jit(solution)/shard_map/all_to_all | solution.py:75
  122.5 21.5 %copy-start.13 = (f32[1,128,1024]{2,1,0:T(8,128)S(1)}, f32[1,128,1024]{2,1,0:T(8,128)}, u32[]{:S(2)}) copy-start(f32[1,128,1024]{2,1,0:T(8,128)} %get-tuple-element.39) | copy-start | bytes 1572868
  122.5 21.5 %copy-start.15 = (f32[1,128,1024]{2,1,0:T(8,128)S(1)}, f32[1,128,1024]{2,1,0:T(8,128)}, u32[]{:S(2)}) copy-start(f32[1,128,1024]{2,1,0:T(8,128)} %copy-done.14) | copy-start | bytes 1572868
  122.5 21.5 %collective-permute-start.1 = (f32[3,6,1024]{2,1,0:T(8,128)S(1)}, f32[3,6,1024]{2,1,0:T(8,128)S(1)}, u32[]{:S(2)}, u32[]{:S(2)}) collective-permute-start(f32[3,6,1024]{2,1,0:T(8,128)S(1)} %slice.160), channel_id=1, source_target_pairs={{8,0},{16,8},{24,16},{9,1},{17,9},{25,17},{10,2},{18,10},{26,18},{... | collective-permute-start | bytes 221192 | tf_op jit(solution)/shard_map/ppermute | solution.py:71
  126.8 17.2 %copy-start.30 = (f32[3,1024]{1,0:T(4,128)S(1)}, f32[3,1024]{1,0:T(4,128)}, u32[]{:S(2)}) copy-start(f32[3,1024]{1,0:T(4,128)} %copy-done.29) | copy-start | bytes 36868
  126.9 17.3 %copy-start.32 = (f32[3,1024]{1,0:T(4,128)S(1)}, f32[3,1024]{1,0:T(4,128)}, u32[]{:S(2)}) copy-start(f32[3,1024]{1,0:T(4,128)} %copy-done.31) | copy-start | bytes 36868
  126.9 17.3 %copy-start.34 = (f32[3,1024]{1,0:T(4,128)S(1)}, f32[3,1024]{1,0:T(4,128)}, u32[]{:S(2)}) copy-start(f32[3,1024]{1,0:T(4,128)} %copy-done.33) | copy-start | bytes 36868
  126.9 17.3 %copy-start.36 = (f32[3,1,1024]{2,0,1:T(4,128)S(1)}, f32[3,1,1024]{2,0,1:T(4,128)}, u32[]{:S(2)}) copy-start(f32[3,1,1024]{2,0,1:T(4,128)} %copy-done.35) | copy-start | bytes 36868
  (19 other events, 23.2 us)
Sparse Core Ops, SparseCore 0:
  20.8 49.0 reduce-scatter.1
  78.9 30.3 all-gather.2
  114.2 59.5 all-reduce.1
  175.7 27.0 all-gather.4

commit v2 on v1

--- a/solution.py
+++ b/solution.py
@@ -3,6 +3,8 @@
 import jax
 import jax.numpy as jnp
 from jax import lax
+from jax.experimental import pallas as pl
+from jax.experimental.pallas import tpu as pltpu
 from jax.sharding import PartitionSpec as P
 
 BF16 = jnp.bfloat16
@@ -133,9 +135,585 @@
     return (grad_features, grad_kernel, grad_filter, grad_weight)
 
 
+MESH = pl.DeviceIdType.MESH
+EDGE = 16
+NEXT_EDGE = 8
+TILE = 128
+ROWS = 256
+W_SLOTS = 3
+
+
+def fused_kernel(
+    features,
+    short_kernel,
+    long_filter,
+    out_weight,
+    grad_out,
+    ahead_high,
+    ahead_low,
+    back_high,
+    back_low,
+    grad_features,
+    grad_kernel,
+    grad_filter,
+    all_grad_out,
+    all_mixed,
+    w_buf,
+    pair_out,
+    pair_in,
+    partials,
+    line_out,
+    line_in,
+    edge_in,
+    extended,
+    conv,
+    filter_out,
+    gated_out,
+    grad_long_out,
+    filter_wide,
+    gated_wide,
+    grad_wide,
+    filter_spec,
+    gated_spec,
+    grad_spec,
+    prod_high,
+    prod_low,
+    long_send,
+    long_recv,
+    back_send,
+    back_recv,
+    lag_send,
+    lag_recv,
+    mixed,
+    grad_mixed,
+    grad_conv,
+    next_edge_in,
+    kernel_parts,
+    w_sem,
+    local_sem,
+    pair_sems,
+    line_sems,
+    edge_sems,
+    next_sems,
+    exchange_sems,
+    mixed_sems,
+    forward_sems,
+):
+    me_ctx, me_ch = lax.axis_index("ctx"), lax.axis_index("ch")
+    n_ctx, lines = lax.axis_size("ctx"), lax.axis_size("ch") // 2
+    core, z = lax.rem(me_ch, 2), me_ch // 2
+    block_len, chans = grad_out.shape
+    taps = short_kernel.shape[1]
+    part = chans // n_ctx
+    length = n_ctx * block_len
+    hops = [k % lines for k in range(1, lines + 1)]
+
+    def column(index):
+        return pl.ds(pl.multiple_of(index * TILE, TILE), TILE)
+
+    def token_rows(index):
+        return pl.ds(pl.multiple_of(index * block_len, block_len), block_len)
+
+    def remote(src, dst, sems, index, ctx, ch):
+        return pltpu.make_async_remote_copy(
+            src_ref=src,
+            dst_ref=dst,
+            send_sem=sems.at[0, index],
+            recv_sem=sems.at[1, index],
+            device_id={"ctx": ctx, "ch": ch},
+            device_id_type=MESH,
+        )
+
+    weight_steps = []
+    for k in hops:
+        target = lax.rem(z + k, lines) * 2
+        weight_steps += [target + 1 - core, target + core]
+
+    def weight_copy(step):
+        slot = step % W_SLOTS
+        start = pl.multiple_of(weight_steps[step] * chans, chans)
+        return pltpu.make_async_copy(
+            out_weight.at[pl.ds(start, chans), :], w_buf.at[slot], w_sem.at[slot]
+        )
+
+    for step in range(W_SLOTS):
+        weight_copy(step).start()
+
+    barrier = pltpu.get_barrier_semaphore()
+    group = me_ctx * lines + z
+    for distance in range(1, n_ctx * lines):
+        other = lax.rem(group + distance, n_ctx * lines)
+        pl.semaphore_signal(
+            barrier,
+            inc=1,
+            device_id={"ctx": other // lines, "ch": lax.rem(other, lines) * 2 + core},
+            device_id_type=MESH,
+        )
+    pl.semaphore_signal(
+        barrier, inc=1, device_id={"ctx": me_ctx, "ch": z * 2 + 1 - core}, device_id_type=MESH
+    )
+
+    def stage_filter(tile, carry):
+        per_part = part // TILE
+        filter_out[tile // per_part, :, column(lax.rem(tile, per_part))] = long_filter[
+            :, column(tile)
+        ]
+        return carry
+
+    lax.fori_loop(0, chans // TILE, stage_filter, 0)
+    filter_wide[token_rows(me_ctx), :] = filter_out[me_ctx]
+    pl.semaphore_wait(barrier, n_ctx * lines)
+
+    def exchange(number, src_at, dst):
+        copies = []
+        for distance in range(1, n_ctx):
+            peer = lax.rem(me_ctx + distance, n_ctx)
+            copies.append(
+                remote(
+                    src_at(peer),
+                    dst,
+                    exchange_sems.at[number],
+                    distance - 1,
+                    peer,
+                    me_ch,
+                )
+            )
+        for copy in copies:
+            copy.start()
+        return copies
+
+    def arrived(copies):
+        for copy in copies:
+            copy.wait_recv()
+
+    edge_copy = remote(
+        features.at[:, pl.ds(block_len - EDGE, EDGE), :],
+        edge_in,
+        edge_sems,
+        0,
+        lax.rem(me_ctx + 1, n_ctx),
+        me_ch,
+    )
+    edge_copy.start()
+    filter_copies = exchange(0, lambda peer: filter_out.at[peer], filter_wide.at[token_rows(me_ctx)])
+
+    pair_copies, line_copies = [], []
+
+    def finish_hop(index):
+        pair_copies[index].wait_recv()
+        if hops[index] == 0:
+            partials[index] = partials[index] + pair_in[index].astype(F32)
+            return
+        line_out[index] = (partials[index] + pair_in[index].astype(F32)).astype(BF16)
+        copy = remote(
+            line_out.at[index],
+            line_in.at[index],
+            line_sems,
+            index,
+            me_ctx,
+            lax.rem(z + hops[index], lines) * 2 + core,
+        )
+        copy.start()
+        line_copies.append(copy)
+
+    for step in range(2 * lines):
+        index = step // 2
+        slot = step % W_SLOTS
+        weight_copy(step).wait()
+
+        def project(tile, carry, step=step, index=index, slot=slot):
+            rows = pl.ds(pl.multiple_of(tile * ROWS, ROWS), ROWS)
+            value = lax.dot_general(
+                grad_out[...],
+                w_buf[slot, rows, :],
+                (((1,), (1,)), ((), ())),
+                preferred_element_type=F32,
+            )
+            if step % 2 == 0:
+                pair_out[index, :, rows] = value.astype(BF16)
+            else:
+                partials[index, :, rows] = value
+            return carry
+
+        lax.fori_loop(0, chans // ROWS, project, 0)
+        if step + W_SLOTS < 2 * lines:
+            weight_copy(step + W_SLOTS).start()
+        if step % 2 == 0:
+            copy = remote(
+                pair_out.at[index], pair_in.at[index], pair_sems, index, me_ctx, z * 2 + 1 - core
+            )
+            copy.start()
+            pair_copies.append(copy)
+            if index >= 1:
+                finish_hop(index - 1)
+
+    edge_copy.wait_recv()
+
+    def convolve(tile, carry):
+        cols = column(tile)
+        totals = []
+        for branch in range(3):
+            edge = edge_in[branch, :, cols].astype(F32)
+            extended[branch, 0:EDGE, cols] = jnp.where(me_ctx > 0, edge, 0.0)
+            extended[branch, EDGE : EDGE + block_len, cols] = features[branch, :, cols].astype(F32)
+            total = None
+            for tap in range(taps):
+                term = (
+                    short_kernel[branch, tap : tap + 1, cols]
+                    * extended[branch, EDGE - tap : EDGE - tap + block_len, cols]
+                )
+                total = term if total is None else total + term
+            conv[branch, :, cols] = total
+            totals.append(total)
+        per_part = part // TILE
+        gated_out[tile // per_part, :, column(lax.rem(tile, per_part))] = (
+            totals[1] * totals[2]
+        ).astype(BF16)
+        return carry
+
+    lax.fori_loop(0, chans // TILE, convolve, 0)
+    gated_copies = exchange(1, lambda peer: gated_out.at[peer], gated_wide.at[token_rows(me_ctx)])
+    gated_wide[token_rows(me_ctx), :] = gated_out[me_ctx]
+    finish_hop(lines - 1)
+    own_grad_out = pltpu.make_async_copy(grad_out, all_grad_out.at[me_ctx], local_sem.at[0])
+    own_grad_out.start()
+
+    def transform(source, target):
+        def body(tile, carry):
+            rows = pl.ds(pl.multiple_of(tile * ROWS, ROWS), ROWS)
+            target[rows, :] = to_spectrum(ahead_high[rows, :], ahead_low[rows, :], source[...])
+            return carry
+
+        lax.fori_loop(0, 2 * length // ROWS, body, 0)
+
+    def multiply(first, second, conjugate):
+        step_rows = 32
+
+        def body(tile, carry):
+            upper = pl.ds(pl.multiple_of(tile * step_rows, step_rows), step_rows)
+            lower = pl.ds(pl.multiple_of(length + tile * step_rows, step_rows), step_rows)
+            first_real, first_imag = first[upper, :], first[lower, :]
+            second_real, second_imag = second[upper, :], second[lower, :]
+            row = lax.broadcasted_iota(jnp.int32, first_real.shape, 0) + tile * step_rows
+            edge = row == 0
+            real_real = first_real * second_real
+            imag_imag = first_imag * second_imag
+            if conjugate:
+                real_part = real_real + imag_imag
+                imag_part = first_real * second_imag - first_imag * second_real
+            else:
+                real_part = real_real - imag_imag
+                imag_part = first_real * second_imag + first_imag * second_real
+            for rows, value in (
+                (upper, jnp.where(edge, real_real, real_part)),
+                (lower, jnp.where(edge, imag_imag, imag_part)),
+            ):
+                high = value.astype(BF16)
+                prod_high[rows, :] = high
+                prod_low[rows, :] = (value - high.astype(F32)).astype(BF16)
+            return carry
+
+        lax.fori_loop(0, length // step_rows, body, 0)
+
+    def invert(target):
+        def body(tile, carry):
+            rows = token_rows(tile)
+            high, low = back_high[rows, :], back_low[rows, :]
+            target[tile] = (
+                jnp.dot(high, prod_high[...], preferred_element_type=F32)
+                + jnp.dot(low, prod_high[...], preferred_element_type=F32)
+                + jnp.dot(high, prod_low[...], preferred_element_type=F32)
+            ).astype(BF16)
+            return carry
+
+        lax.fori_loop(0, n_ctx, body, 0)
+
+    arrived(filter_copies)
+    transform(filter_wide, filter_spec)
+    arrived(gated_copies)
+    transform(gated_wide, gated_spec)
+    multiply(filter_spec, gated_spec, False)
+    invert(long_send)
+    long_copies = exchange(2, lambda peer: long_send.at[peer], long_recv.at[me_ctx])
+    long_recv[me_ctx] = long_send[me_ctx]
+    grad_out_copies = exchange(3, lambda peer: grad_out, all_grad_out.at[me_ctx])
+
+    arrived(long_copies)
+
+    def per_part_view(ref, tile):
+        per_part = part // TILE
+        return ref[tile // per_part, :, column(lax.rem(tile, per_part))].astype(F32)
+
+    def mix(tile, carry):
+        cols = column(tile)
+        mixed[:, cols] = (conv[0, :, cols] * per_part_view(long_recv, tile)).astype(BF16)
+        return carry
+
+    lax.fori_loop(0, chans // TILE, mix, 0)
+
+    def mixed_copy(k):
+        return pltpu.make_async_remote_copy(
+            src_ref=mixed,
+            dst_ref=all_mixed.at[core, me_ctx],
+            send_sem=mixed_sems.at[0, k],
+            recv_sem=mixed_sems.at[1, me_ctx],
+            device_id={"ctx": z, "ch": lax.rem(z + k, lines) * 2 + core},
+            device_id_type=MESH,
+        )
+
+    own_mixed = pltpu.make_async_copy(mixed, all_mixed.at[core, me_ctx], local_sem.at[1])
+    mine = me_ctx == z
+    for k in range(1, lines):
+        mixed_copy(k).start()
+
+    @pl.when(mine)
+    def _():
+        own_mixed.start()
+
+    @pl.when(jnp.logical_not(mine))
+    def _():
+        mixed_copy(0).start()
+
+    for copy in line_copies:
+        copy.wait_recv()
+
+    def take_grad(tile, carry):
+        cols = column(tile)
+        total = partials[lines - 1, :, cols]
+        for index in range(lines - 1):
+            total = total + line_in[index, :, cols].astype(F32)
+        grad_mixed[:, cols] = total
+        per_part = part // TILE
+        grad_long_out[tile // per_part, :, column(lax.rem(tile, per_part))] = (
+            total * conv[0, :, cols]
+        ).astype(BF16)
+        return carry
+
+    lax.fori_loop(0, chans // TILE, take_grad, 0)
+    grad_copies = exchange(
+        4, lambda peer: grad_long_out.at[peer], grad_wide.at[token_rows(me_ctx)]
+    )
+    grad_wide[token_rows(me_ctx), :] = grad_long_out[me_ctx]
+    arrived(grad_copies)
+    transform(grad_wide, grad_spec)
+    multiply(filter_spec, grad_spec, True)
+    invert(back_send)
+    back_copies = exchange(5, lambda peer: back_send.at[peer], back_recv.at[me_ctx])
+    back_recv[me_ctx] = back_send[me_ctx]
+    multiply(gated_spec, grad_spec, True)
+    invert(lag_send)
+    lag_copies = exchange(6, lambda peer: lag_send.at[peer], lag_recv.at[me_ctx])
+    lag_recv[me_ctx] = lag_send[me_ctx]
+    arrived(back_copies)
+
+    def conv_gradient(tile, carry):
+        cols = column(tile)
+        back = per_part_view(back_recv, tile)
+        grad_conv[0, 0:block_len, cols] = grad_mixed[:, cols] * per_part_view(long_recv, tile)
+        grad_conv[1, 0:block_len, cols] = back * conv[2, :, cols]
+        grad_conv[2, 0:block_len, cols] = back * conv[1, :, cols]
+        return carry
+
+    lax.fori_loop(0, chans // TILE, conv_gradient, 0)
+    next_copy = remote(
+        grad_conv.at[:, pl.ds(0, NEXT_EDGE), :],
+        next_edge_in,
+        next_sems,
+        0,
+        lax.rem(me_ctx + n_ctx - 1, n_ctx),
+        me_ch,
+    )
+    next_copy.start()
+
+    def tap_gradient(tile, carry):
+        cols = column(tile)
+        for branch in range(3):
+            values = grad_conv[branch, 0:block_len, cols]
+            for tap in range(taps):
+                term = values * extended[branch, EDGE - tap : EDGE - tap + block_len, cols]
+                kernel_parts[me_ctx, branch, tap : tap + 1, cols] = jnp.sum(
+                    term, axis=0, keepdims=True
+                )
+            kernel_parts[me_ctx, branch, taps : taps + 1, cols] = jnp.zeros((1, TILE), F32)
+        return carry
+
+    lax.fori_loop(0, chans // TILE, tap_gradient, 0)
+    kernel_copies = exchange(7, lambda peer: kernel_parts.at[me_ctx], kernel_parts.at[me_ctx])
+    next_copy.wait()
+
+    def feature_gradient(tile, carry):
+        cols = column(tile)
+        for branch in range(3):
+            grad_conv[branch, block_len : block_len + NEXT_EDGE, cols] = jnp.where(
+                me_ctx < n_ctx - 1, next_edge_in[branch, :, cols], 0.0
+            )
+            total = None
+            for tap in range(taps):
+                term = (
+                    short_kernel[branch, tap : tap + 1, cols]
+                    * grad_conv[branch, tap : tap + block_len, cols]
+                )
+                total = term if total is None else total + term
+            grad_features[branch, :, cols] = total.astype(BF16)
+        return carry
+
+    lax.fori_loop(0, chans // TILE, feature_gradient, 0)
+
+    forward_copies = []
+    for source in range(n_ctx):
+        here = jnp.logical_and(mine, me_ctx == source)
+
+        @pl.when(here)
+        def _():
+            own_mixed.wait()
+
+        @pl.when(jnp.logical_not(here))
+        def _(source=source):
+            slot = all_mixed.at[core, source]
+            remote(mixed, slot, mixed_sems, source, me_ctx, z * 2 + 1 - core).wait_recv()
+
+        copy = remote(
+            all_mixed.at[core, source],
+            all_mixed.at[core, source],
+            forward_sems,
+            source,
+            me_ctx,
+            z * 2 + 1 - core,
+        )
+        copy.start()
+        forward_copies.append(copy)
+
+    arrived(lag_copies)
+
+    def filter_gradient(tile, carry):
+        grad_filter[:, column(tile)] = per_part_view(lag_recv, tile)
+        return carry
+
+    lax.fori_loop(0, chans // TILE, filter_gradient, 0)
+    arrived(kernel_copies)
+    total = kernel_parts[0]
+    for index in range(1, n_ctx):
+        total = total + kernel_parts[index]
+    grad_kernel[...] = total[:, :taps, :]
+    arrived(grad_out_copies)
+    own_grad_out.wait()
+    for copy in forward_copies:
+        copy.wait()
+    edge_copy.wait_send()
+    for copies in (
+        filter_copies,
+        gated_copies,
+        long_copies,
+        grad_out_copies,
+        grad_copies,
+        back_copies,
+        lag_copies,
+        kernel_copies,
+        pair_copies,
+        line_copies,
+    ):
+        for copy in copies:
+            copy.wait_send()
+    for k in range(1, lines):
+        mixed_copy(k).wait_send()
+
+    @pl.when(jnp.logical_not(mine))
+    def _():
+        mixed_copy(0).wait_send()
+
+
+def fused(features, short_kernel, long_filter, out_weight, grad_out):
+    block_len, chans = grad_out.shape
+    taps = short_kernel.shape[1]
+    n_ctx, lines = lax.axis_size("ctx"), lax.axis_size("ch") // 2
+    part, length = chans // n_ctx, n_ctx * block_len
+    tables = [jnp.asarray(table) for table in fourier_tables(length)]
+    in_vmem = pl.BlockSpec(memory_space=pltpu.VMEM)
+    in_place = pl.BlockSpec(memory_space=pl.ANY)
+    staged = pltpu.VMEM((n_ctx, block_len, part), BF16)
+    wide = pltpu.VMEM((length, part), BF16)
+    spectra = pltpu.VMEM((2 * length, part), F32)
+    blocks = pltpu.VMEM((lines, block_len, chans), BF16)
+    scratch = [
+        pltpu.VMEM((W_SLOTS, chans, chans), BF16),
+        blocks,
+        blocks,
+        pltpu.VMEM((lines, block_len, chans), F32),
+        blocks,
+        blocks,
+        pltpu.VMEM((3, EDGE, chans), BF16),
+        pltpu.VMEM((3, EDGE + block_len, chans), F32),
+        pltpu.VMEM((3, block_len, chans), F32),
+        staged,
+        staged,
+        staged,
+        wide,
+        wide,
+        wide,
+        spectra,
+        spectra,
+        spectra,
+        pltpu.VMEM((2 * length, part), BF16),
+        pltpu.VMEM((2 * length, part), BF16),
+        staged,
+        staged,
+        staged,
+        staged,
+        staged,
+        staged,
+        pltpu.VMEM((block_len, chans), BF16),
+        pltpu.VMEM((block_len, chans), F32),
+        pltpu.VMEM((3, block_len + NEXT_EDGE, chans), F32),
+        pltpu.VMEM((3, NEXT_EDGE, chans), F32),
+        pltpu.VMEM((n_ctx, 3, taps + 1, chans), F32),
+        pltpu.SemaphoreType.DMA((W_SLOTS,)),
+        pltpu.SemaphoreType.DMA((2,)),
+        pltpu.SemaphoreType.DMA((2, lines)),
+        pltpu.SemaphoreType.DMA((2, lines)),
+        pltpu.SemaphoreType.DMA((2, 1)),
+        pltpu.SemaphoreType.DMA((2, 1)),
+        pltpu.SemaphoreType.DMA((8, 2, n_ctx - 1)),
+        pltpu.SemaphoreType.DMA((2, max(lines, n_ctx))),
+        pltpu.SemaphoreType.DMA((2, n_ctx)),
+    ]
+    grad_features, grad_kernel, grad_filter, all_grad_out, all_mixed = pl.pallas_call(
+        fused_kernel,
+        out_shape=[
+            jax.ShapeDtypeStruct(features.shape, BF16),
+            jax.ShapeDtypeStruct(short_kernel.shape, F32),
+            jax.ShapeDtypeStruct(long_filter.shape, F32),
+            jax.ShapeDtypeStruct((n_ctx, block_len, chans), BF16),
+            jax.ShapeDtypeStruct((2, n_ctx, block_len, chans), BF16),
+        ],
+        in_specs=[in_vmem, in_vmem, in_vmem, in_place] + [in_vmem] * 5,
+        out_specs=[in_vmem, in_vmem, in_vmem, in_place, in_place],
+        scratch_shapes=scratch,
+        compiler_params=pltpu.CompilerParams(
+            collective_id=0, has_side_effects=True, vmem_limit_bytes=56 * 1024 * 1024
+        ),
+        cost_estimate=pl.CostEstimate(
+            flops=8 * 10**9, bytes_accessed=28 * 2**20, transcendentals=0
+        ),
+    )(features, short_kernel, long_filter, out_weight, grad_out, *tables)
+    grad_weight = jnp.einsum(
+        "ktn,tc->knc",
+        all_mixed.reshape(2, length, chans),
+        all_grad_out.reshape(length, chans),
+        preferred_element_type=F32,
+    ).reshape(2 * chans, chans)
+    return (grad_features, grad_kernel, grad_filter, grad_weight)
+
+
 def solution(mesh):
+    n_ctx, n_ch = mesh.shape["ctx"], mesh.shape["ch"]
+
+    def local(features, short_kernel, long_filter, out_weight, grad_out):
+        aligned = grad_out.shape[1] % (TILE * n_ctx) == 0 and grad_out.shape[1] % ROWS == 0
+        body = fused if n_ch == 2 * n_ctx and aligned else plain
+        return body(features, short_kernel, long_filter, out_weight, grad_out)
+
     return jax.shard_map(
-        plain,
+        local,
         mesh=mesh,
         in_specs=(
             P(None, "ctx", "ch"),

time: 221 us -> 92.8 us (0.42)
  the two profiles are of different devices: /device:TPU:7 before, /device:TPU:0 now
where the time goes in v2:
time: 92.8 us; the launch traced here: 92.6 us
  Pallas kernels  80.9 us (87%)
  matrix products  5.74 us (6%)
  local copies, waits for them, and re-layouts  5.28 us (6%)
    pallas_call x1, Pallas kernels, fused(): pl.pallas_call(fused_kernel, out_shape=[jax.ShapeDtypeStruct(features.sha...  80.9 us
    dot_general x1, matrix products, fused(): jnp.einsum('ktn,tc->knc', all_mixed.reshape(2, length, chans), all_grad_o...  5.74 us
    reshape x1, local copies, waits for them, and re-layouts, fused(): all_mixed.reshape(2, length, chans)  2.95 us
    unnamed x11, local copies, waits for them, and re-layouts  2.33 us

profile of v2, /device:TPU:0, one launch (start us, length us, event | category | flops | bytes accessed | tf_op | source)
XLA Modules:
  0.0 92.6 jit_solution(3446128276383667595)
XLA Ops:
  0.6 80.9 %shard_map.120 = (bf16[3,128,1024]{2,1,0:T(8,128)(2,1)}, f32[3,7,1024]{2,1,0:T(8,128)}, f32[128,1024]{1,0:T(8,128)}, bf16[4,128,1024]{2,1,0:T(8,128)(2,1)}, bf16[2,4,128,1024]{3,2,1,0:T(8,128)(2,1)}) custom-call(bf16[3,128,1024]{2,1,0:T(8,128)(2,1)} %features.1, f32[3,7,1024]{2,1,0:T(8,128)} %short_kernel.1, bf16[128,1024]{1,0:T(8,128)(2,1)} %long_filter.1, ...), custom_call_target="tpu_custom_call" | custom-call | flops 8000000000 | bytes 29360128 | tf_op jit(solution)/shard_map/pallas_call | solution.py:679
  81.5 0.0 copy-start.3
  81.5 2.9 %copy.13 = bf16[2,512,1024]{1,2,0:T(8,128)(2,1)S(1)} copy(bf16[2,512,1024]{2,1,0:T(8,128)(2,1)} %bitcast.7) | data formatting | bytes 4194304 | tf_op jit(solution)/shard_map/reshape | solution.py:700
  84.5 0.0 copy-done.3
  84.5 0.0 copy-start
  84.5 0.0 copy-start.2
  84.5 5.7 %fusion = f32[2048,1024]{1,0:T(8,128)} fusion(bf16[2048,512]{1,0:T(8,128)(2,1)S(1)} %bitcast.8, bf16[512,1024]{1,0:T(8,128)(2,1)S(1)} %bitcast.9), kind=kOutput, calls=%fused_computation | convolution fusion | flops 2147483648 | bytes 11534336 | tf_op jit(solution)/shard_map/ktn,tc->knc/dot_general | solution.py:698
  90.3 0.0 copy-done
  90.3 0.0 copy-start.1
  90.3 0.9 copy.17
  91.2 0.0 copy-done.2
  91.2 0.6 copy.18
  91.8 0.0 copy-done.1
  91.8 0.8 copy.19
Async XLA Ops:
  81.5 3.0 %copy-start.3 = (bf16[4,128,1024]{2,1,0:T(8,128)(2,1)S(1)}, bf16[4,128,1024]{2,1,0:T(8,128)(2,1)}, u32[]{:S(2)}) copy-start(bf16[4,128,1024]{2,1,0:T(8,128)(2,1)} %get-tuple-element.13) | copy-start | bytes 3145732
  84.5 5.8 %copy-start = (bf16[3,128,1024]{2,1,0:T(8,128)(2,1)S(1)}, bf16[3,128,1024]{2,1,0:T(8,128)(2,1)}, u32[]{:S(2)}) copy-start(bf16[3,128,1024]{2,1,0:T(8,128)(2,1)} %get-tuple-element.18) | copy-start | bytes 2359300
  84.5 6.6 %copy-start.2 = (f32[3,7,1024]{2,1,0:T(8,128)S(1)}, f32[3,7,1024]{2,1,0:T(8,128)}, u32[]{:S(2)}) copy-start(f32[3,7,1024]{2,1,0:T(8,128)} %get-tuple-element.19) | copy-start | bytes 258052
  90.3 1.5 %copy-start.1 = (f32[128,1024]{1,0:T(8,128)S(1)}, f32[128,1024]{1,0:T(8,128)}, u32[]{:S(2)}) copy-start(f32[128,1024]{1,0:T(8,128)} %get-tuple-element.20) | copy-start | bytes 1572868

commit v3 on v2

--- a/solution.py
+++ b/solution.py
@@ -184,7 +184,7 @@
     back_recv,
     lag_send,
     lag_recv,
-    mixed,
+    line_mixed,
     grad_mixed,
     grad_conv,
     next_edge_in,
@@ -196,7 +196,8 @@
     edge_sems,
     next_sems,
     exchange_sems,
-    mixed_sems,
+    chain_sems,
+    relay_sems,
     forward_sems,
 ):
     me_ctx, me_ch = lax.axis_index("ctx"), lax.axis_index("ch")
@@ -240,18 +241,13 @@
         weight_copy(step).start()
 
     barrier = pltpu.get_barrier_semaphore()
-    group = me_ctx * lines + z
-    for distance in range(1, n_ctx * lines):
-        other = lax.rem(group + distance, n_ctx * lines)
+    greeted = [(lax.rem(me_ctx + d, n_ctx), me_ch) for d in range(1, n_ctx)]
+    greeted += [(me_ctx, lax.rem(z + d, lines) * 2 + core) for d in range(1, lines)]
+    greeted.append((me_ctx, z * 2 + 1 - core))
+    for ctx, ch in greeted:
         pl.semaphore_signal(
-            barrier,
-            inc=1,
-            device_id={"ctx": other // lines, "ch": lax.rem(other, lines) * 2 + core},
-            device_id_type=MESH,
-        )
-    pl.semaphore_signal(
-        barrier, inc=1, device_id={"ctx": me_ctx, "ch": z * 2 + 1 - core}, device_id_type=MESH
-    )
+            barrier, inc=1, device_id={"ctx": ctx, "ch": ch}, device_id_type=MESH
+        )
 
     def stage_filter(tile, carry):
         per_part = part // TILE
@@ -262,7 +258,7 @@
 
     lax.fori_loop(0, chans // TILE, stage_filter, 0)
     filter_wide[token_rows(me_ctx), :] = filter_out[me_ctx]
-    pl.semaphore_wait(barrier, n_ctx * lines)
+    pl.semaphore_wait(barrier, len(greeted))
 
     def exchange(number, src_at, dst):
         copies = []
@@ -446,36 +442,76 @@
 
     def mix(tile, carry):
         cols = column(tile)
-        mixed[:, cols] = (conv[0, :, cols] * per_part_view(long_recv, tile)).astype(BF16)
+        line_mixed[z, :, cols] = (conv[0, :, cols] * per_part_view(long_recv, tile)).astype(BF16)
         return carry
 
     lax.fori_loop(0, chans // TILE, mix, 0)
 
-    def mixed_copy(k):
+    def chain_copy(sign, distance):
+        block = line_mixed.at[z - sign * (distance - 1)]
+        way = 0 if sign > 0 else 1
+        return remote(
+            block, block, chain_sems.at[way], distance - 1, me_ctx, (z + sign) * 2 + core
+        )
+
+    def chain_sends(sign, distance):
+        first, after = z - sign * (distance - 1), z + sign
+        inside = jnp.logical_and(first >= 0, first < lines)
+        return jnp.logical_and(inside, jnp.logical_and(after >= 0, after < lines))
+
+    def chain_receives(sign, distance):
+        first = z - sign * distance
+        return jnp.logical_and(first >= 0, first < lines)
+
+    own_relay = pltpu.make_async_copy(
+        line_mixed.at[me_ctx], all_mixed.at[core, me_ctx], local_sem.at[1]
+    )
+
+    def relay_copy(block):
         return pltpu.make_async_remote_copy(
-            src_ref=mixed,
+            src_ref=line_mixed.at[block],
             dst_ref=all_mixed.at[core, me_ctx],
-            send_sem=mixed_sems.at[0, k],
-            recv_sem=mixed_sems.at[1, me_ctx],
-            device_id={"ctx": z, "ch": lax.rem(z + k, lines) * 2 + core},
+            send_sem=relay_sems.at[0, block],
+            recv_sem=relay_sems.at[1, me_ctx],
+            device_id={"ctx": block, "ch": me_ch},
             device_id_type=MESH,
         )
 
-    own_mixed = pltpu.make_async_copy(mixed, all_mixed.at[core, me_ctx], local_sem.at[1])
-    mine = me_ctx == z
-    for k in range(1, lines):
-        mixed_copy(k).start()
-
-    @pl.when(mine)
-    def _():
-        own_mixed.start()
-
-    @pl.when(jnp.logical_not(mine))
-    def _():
-        mixed_copy(0).start()
+    def relay(block):
+        @pl.when(block == me_ctx)
+        def _():
+            own_relay.start()
+
+        @pl.when(block != me_ctx)
+        def _():
+            relay_copy(block).start()
+
+    def chain_start(distance):
+        for sign in (1, -1):
+
+            @pl.when(chain_sends(sign, distance))
+            def _(sign=sign):
+                chain_copy(sign, distance).start()
+
+    def chain_take(distance):
+        for sign in (1, -1):
+
+            @pl.when(chain_receives(sign, distance))
+            def _(sign=sign):
+                chain_copy(sign, distance).wait_recv()
+
+        if distance + 1 < lines:
+            chain_start(distance + 1)
+        for sign in (1, -1):
+
+            @pl.when(chain_receives(sign, distance))
+            def _(sign=sign):
+                relay(z - sign * distance)
 
     for copy in line_copies:
         copy.wait_recv()
+    chain_start(1)
+    relay(z)
 
     def take_grad(tile, carry):
         cols = column(tile)
@@ -496,6 +532,7 @@
     grad_wide[token_rows(me_ctx), :] = grad_long_out[me_ctx]
     arrived(grad_copies)
     transform(grad_wide, grad_spec)
+    chain_take(1)
     multiply(filter_spec, grad_spec, True)
     invert(back_send)
     back_copies = exchange(5, lambda peer: back_send.at[peer], back_recv.at[me_ctx])
@@ -504,6 +541,8 @@
     invert(lag_send)
     lag_copies = exchange(6, lambda peer: lag_send.at[peer], lag_recv.at[me_ctx])
     lag_recv[me_ctx] = lag_send[me_ctx]
+    for distance in range(2, lines - 1):
+        chain_take(distance)
     arrived(back_copies)
 
     def conv_gradient(tile, carry):
@@ -539,6 +578,7 @@
 
     lax.fori_loop(0, chans // TILE, tap_gradient, 0)
     kernel_copies = exchange(7, lambda peer: kernel_parts.at[me_ctx], kernel_parts.at[me_ctx])
+    chain_take(lines - 1)
     next_copy.wait()
 
     def feature_gradient(tile, carry):
@@ -561,16 +601,14 @@
 
     forward_copies = []
     for source in range(n_ctx):
-        here = jnp.logical_and(mine, me_ctx == source)
-
-        @pl.when(here)
+        @pl.when(me_ctx == source)
         def _():
-            own_mixed.wait()
-
-        @pl.when(jnp.logical_not(here))
+            own_relay.wait()
+
+        @pl.when(me_ctx != source)
         def _(source=source):
             slot = all_mixed.at[core, source]
-            remote(mixed, slot, mixed_sems, source, me_ctx, z * 2 + 1 - core).wait_recv()
+            remote(line_mixed.at[0], slot, relay_sems, source, me_ctx, me_ch).wait_recv()
 
         copy = remote(
             all_mixed.at[core, source],
@@ -614,12 +652,55 @@
     ):
         for copy in copies:
             copy.wait_send()
-    for k in range(1, lines):
-        mixed_copy(k).wait_send()
-
-    @pl.when(jnp.logical_not(mine))
+    for distance in range(1, lines):
+        for sign in (1, -1):
+
+            @pl.when(chain_sends(sign, distance))
+            def _(sign=sign, distance=distance):
+                chain_copy(sign, distance).wait_send()
+
+    for block in range(lines):
+
+        @pl.when(me_ctx != block)
+        def _(block=block):
+            relay_copy(block).wait_send()
+
+
+def product_kernel(
+    mixed_tile,
+    all_grad_out,
+    features_from,
+    kernel_from,
+    filter_from,
+    grad_weight,
+    features_to,
+    kernel_to,
+    filter_to,
+    sems,
+):
+    step, steps = pl.program_id(0), pl.num_programs(0)
+    pairs = [(features_from, features_to), (kernel_from, kernel_to), (filter_from, filter_to)]
+    copies = [
+        pltpu.make_async_copy(source, target, sems.at[index])
+        for index, (source, target) in enumerate(pairs)
+    ]
+
+    @pl.when(step == 0)
     def _():
-        mixed_copy(0).wait_send()
+        for copy in copies:
+            copy.start()
+
+    grad_weight[...] = lax.dot_general(
+        mixed_tile[0],
+        all_grad_out[...],
+        (((0,), (0,)), ((), ())),
+        preferred_element_type=F32,
+    )
+
+    @pl.when(step == steps - 1)
+    def _():
+        for copy in copies:
+            copy.wait()
 
 
 def fused(features, short_kernel, long_filter, out_weight, grad_out):
@@ -661,7 +742,7 @@
         staged,
         staged,
         staged,
-        pltpu.VMEM((block_len, chans), BF16),
+        blocks,
         pltpu.VMEM((block_len, chans), F32),
         pltpu.VMEM((3, block_len + NEXT_EDGE, chans), F32),
         pltpu.VMEM((3, NEXT_EDGE, chans), F32),
@@ -673,7 +754,8 @@
         pltpu.SemaphoreType.DMA((2, 1)),
         pltpu.SemaphoreType.DMA((2, 1)),
         pltpu.SemaphoreType.DMA((8, 2, n_ctx - 1)),
-        pltpu.SemaphoreType.DMA((2, max(lines, n_ctx))),
+        pltpu.SemaphoreType.DMA((2, 2, lines - 1)),
+        pltpu.SemaphoreType.DMA((2, lines)),
         pltpu.SemaphoreType.DMA((2, n_ctx)),
     ]
     grad_features, grad_kernel, grad_filter, all_grad_out, all_mixed = pl.pallas_call(
@@ -695,12 +777,41 @@
             flops=8 * 10**9, bytes_accessed=28 * 2**20, transcendentals=0
         ),
     )(features, short_kernel, long_filter, out_weight, grad_out, *tables)
-    grad_weight = jnp.einsum(
-        "ktn,tc->knc",
+    per_half = chans // ROWS
+    grad_weight, grad_features, grad_kernel, grad_filter = pl.pallas_call(
+        product_kernel,
+        grid=(2 * per_half,),
+        out_shape=[
+            jax.ShapeDtypeStruct((2 * chans, chans), F32),
+            jax.ShapeDtypeStruct(grad_features.shape, BF16),
+            jax.ShapeDtypeStruct(grad_kernel.shape, F32),
+            jax.ShapeDtypeStruct(grad_filter.shape, F32),
+        ],
+        in_specs=[
+            pl.BlockSpec((1, length, ROWS), lambda i: (i // per_half, 0, lax.rem(i, per_half))),
+            pl.BlockSpec((length, chans), lambda i: (0, 0)),
+            in_place,
+            in_place,
+            in_place,
+        ],
+        out_specs=[
+            pl.BlockSpec((ROWS, chans), lambda i: (i, 0)),
+            in_place,
+            in_place,
+            in_place,
+        ],
+        scratch_shapes=[pltpu.SemaphoreType.DMA((3,))],
+        compiler_params=pltpu.CompilerParams(vmem_limit_bytes=32 * 1024 * 1024),
+        cost_estimate=pl.CostEstimate(
+            flops=4 * 10**9, bytes_accessed=12 * 2**20, transcendentals=0
+        ),
+    )(
         all_mixed.reshape(2, length, chans),
         all_grad_out.reshape(length, chans),
-        preferred_element_type=F32,
-    ).reshape(2 * chans, chans)
+        grad_features,
+        grad_kernel,
+        grad_filter,
+    )
     return (grad_features, grad_kernel, grad_filter, grad_weight)
 
 

time: 92.8 us -> 107 us (1.15)
  the two profiles are of different devices: /device:TPU:0 before, /device:TPU:7 now
where the time goes in v3:
time: 107 us; the launch traced here: 106 us
  Pallas kernels  99.8 us (93%)
  local copies, waits for them, and re-layouts  5.87 us (5%)
    pallas_call x1, Pallas kernels, fused(): pl.pallas_call(fused_kernel, out_shape=[jax.ShapeDtypeStruct(features.sha...  93.3 us
    pallas_call x1, Pallas kernels, fused(): pl.pallas_call(product_kernel, grid=(2 * per_half,), out_shape=[jax.Shape...  6.45 us
    unnamed x10, local copies, waits for them, and re-layouts  5.87 us

profile of v3, /device:TPU:7, one launch (start us, length us, event | category | flops | bytes accessed | tf_op | source)
XLA Modules:
  0.0 106.3 jit_solution(3682959568246508273)
XLA Ops:
  0.6 93.3 %shard_map.120 = (bf16[3,128,1024]{2,1,0:T(8,128)(2,1)}, f32[3,7,1024]{2,1,0:T(8,128)}, f32[128,1024]{1,0:T(8,128)}, bf16[4,128,1024]{2,1,0:T(8,128)(2,1)}, bf16[2,4,128,1024]{3,2,1,0:T(8,128)(2,1)}) custom-call(bf16[3,128,1024]{2,1,0:T(8,128)(2,1)} %features.1, f32[3,7,1024]{2,1,0:T(8,128)} %short_kernel.1, bf16[128,1024]{1,0:T(8,128)(2,1)} %long_filter.1, ...), custom_call_target="tpu_custom_call" | custom-call | flops 8000000000 | bytes 29360128 | tf_op jit(solution)/shard_map/pallas_call | solution.py:761
  94.0 0.0 copy-start
  94.0 1.6 %copy-done = bf16[2,4,128,1024]{3,2,1,0:T(8,128)(2,1)S(1)} copy-done((bf16[2,4,128,1024]{3,2,1,0:T(8,128)(2,1)S(1)}, bf16[2,4,128,1024]{3,2,1,0:T(8,128)(2,1)}, u32[]{:S(2)}) %copy-start) | copy-done | bytes 2097176
  95.6 0.0 copy-start.1
  95.6 1.2 %copy-done.1 = bf16[4,128,1024]{2,1,0:T(8,128)(2,1)S(1)} copy-done((bf16[4,128,1024]{2,1,0:T(8,128)(2,1)S(1)}, bf16[4,128,1024]{2,1,0:T(8,128)(2,1)}, u32[]{:S(2)}) %copy-start.1) | copy-done | bytes 1048600
  96.8 0.0 copy-start.2
  96.8 1.1 %copy-done.2 = bf16[3,128,1024]{2,1,0:T(8,128)(2,1)S(1)} copy-done((bf16[3,128,1024]{2,1,0:T(8,128)(2,1)S(1)}, bf16[3,128,1024]{2,1,0:T(8,128)(2,1)}, u32[]{:S(2)}) %copy-start.2) | copy-done | bytes 786456
  97.9 0.0 copy-start.3
  97.9 1.0 copy-done.3
  99.0 0.0 copy-start.4
  99.0 0.9 copy-done.4
  99.9 6.5 %shard_map.121 = (f32[2048,1024]{1,0:T(8,128)}, bf16[3,128,1024]{2,1,0:T(8,128)(2,1)}, f32[3,7,1024]{2,1,0:T(8,128)}, f32[128,1024]{1,0:T(8,128)}) custom-call(bf16[2,512,1024]{2,1,0:T(8,128)(2,1)S(1)} %bitcast.2, bf16[512,1024]{1,0:T(8,128)(2,1)S(1)} %bitcast.3, bf16[3,128,1024]{2,1,0:T(8,128)(2,1)S(1)} %copy-done.2, f32[3,7,1024]{2,1,0:T(8,128)S(1)} %copy-done.4, ...), custom_call_target="tpu_custom_call" | custom-call | flops 4000000000 | bytes 12582912 | tf_op jit(solution)/shard_map/pallas_call | solution.py:781
Async XLA Ops:
  94.0 1.6 %copy-start = (bf16[2,4,128,1024]{3,2,1,0:T(8,128)(2,1)S(1)}, bf16[2,4,128,1024]{3,2,1,0:T(8,128)(2,1)}, u32[]{:S(2)}) copy-start(bf16[2,4,128,1024]{3,2,1,0:T(8,128)(2,1)} %get-tuple-element.13) | copy-start | bytes 6291460
  95.6 1.2 %copy-start.1 = (bf16[4,128,1024]{2,1,0:T(8,128)(2,1)S(1)}, bf16[4,128,1024]{2,1,0:T(8,128)(2,1)}, u32[]{:S(2)}) copy-start(bf16[4,128,1024]{2,1,0:T(8,128)(2,1)} %get-tuple-element.14) | copy-start | bytes 3145732
  96.8 1.1 %copy-start.2 = (bf16[3,128,1024]{2,1,0:T(8,128)(2,1)S(1)}, bf16[3,128,1024]{2,1,0:T(8,128)(2,1)}, u32[]{:S(2)}) copy-start(bf16[3,128,1024]{2,1,0:T(8,128)(2,1)} %get-tuple-element.15.features_from) | copy-start | bytes 2359300
  97.9 1.0 copy-start.3
  99.0 0.9 copy-start.4

commit v4 on v3

--- a/solution.py
+++ b/solution.py
@@ -185,7 +185,6 @@
     lag_send,
     lag_recv,
     line_mixed,
-    grad_mixed,
     grad_conv,
     next_edge_in,
     kernel_parts,
@@ -508,17 +507,17 @@
             def _(sign=sign):
                 relay(z - sign * distance)
 
+    chain_start(1)
+    relay(z)
     for copy in line_copies:
         copy.wait_recv()
-    chain_start(1)
-    relay(z)
 
     def take_grad(tile, carry):
         cols = column(tile)
         total = partials[lines - 1, :, cols]
         for index in range(lines - 1):
             total = total + line_in[index, :, cols].astype(F32)
-        grad_mixed[:, cols] = total
+        grad_conv[0, 0:block_len, cols] = total * per_part_view(long_recv, tile)
         per_part = part // TILE
         grad_long_out[tile // per_part, :, column(lax.rem(tile, per_part))] = (
             total * conv[0, :, cols]
@@ -530,9 +529,26 @@
         4, lambda peer: grad_long_out.at[peer], grad_wide.at[token_rows(me_ctx)]
     )
     grad_wide[token_rows(me_ctx), :] = grad_long_out[me_ctx]
+
+    def tap_gradient(branches):
+        def body(tile, carry):
+            cols = column(tile)
+            for branch in branches:
+                values = grad_conv[branch, 0:block_len, cols]
+                for tap in range(taps):
+                    term = values * extended[branch, EDGE - tap : EDGE - tap + block_len, cols]
+                    kernel_parts[me_ctx, branch, tap : tap + 1, cols] = jnp.sum(
+                        term, axis=0, keepdims=True
+                    )
+                kernel_parts[me_ctx, branch, taps : taps + 1, cols] = jnp.zeros((1, TILE), F32)
+            return carry
+
+        return body
+
+    lax.fori_loop(0, chans // TILE, tap_gradient((0,)), 0)
+    chain_take(1)
     arrived(grad_copies)
     transform(grad_wide, grad_spec)
-    chain_take(1)
     multiply(filter_spec, grad_spec, True)
     invert(back_send)
     back_copies = exchange(5, lambda peer: back_send.at[peer], back_recv.at[me_ctx])
@@ -548,7 +564,6 @@
     def conv_gradient(tile, carry):
         cols = column(tile)
         back = per_part_view(back_recv, tile)
-        grad_conv[0, 0:block_len, cols] = grad_mixed[:, cols] * per_part_view(long_recv, tile)
         grad_conv[1, 0:block_len, cols] = back * conv[2, :, cols]
         grad_conv[2, 0:block_len, cols] = back * conv[1, :, cols]
         return carry
@@ -564,22 +579,32 @@
     )
     next_copy.start()
 
-    def tap_gradient(tile, carry):
-        cols = column(tile)
-        for branch in range(3):
-            values = grad_conv[branch, 0:block_len, cols]
-            for tap in range(taps):
-                term = values * extended[branch, EDGE - tap : EDGE - tap + block_len, cols]
-                kernel_parts[me_ctx, branch, tap : tap + 1, cols] = jnp.sum(
-                    term, axis=0, keepdims=True
-                )
-            kernel_parts[me_ctx, branch, taps : taps + 1, cols] = jnp.zeros((1, TILE), F32)
-        return carry
-
-    lax.fori_loop(0, chans // TILE, tap_gradient, 0)
+    chain_take(lines - 1)
+    lax.fori_loop(0, chans // TILE, tap_gradient((1, 2)), 0)
     kernel_copies = exchange(7, lambda peer: kernel_parts.at[me_ctx], kernel_parts.at[me_ctx])
-    chain_take(lines - 1)
     next_copy.wait()
+
+    forward_copies = []
+    for source in range(n_ctx):
+        @pl.when(me_ctx == source)
+        def _():
+            own_relay.wait()
+
+        @pl.when(me_ctx != source)
+        def _(source=source):
+            slot = all_mixed.at[core, source]
+            remote(line_mixed.at[0], slot, relay_sems, source, me_ctx, me_ch).wait_recv()
+
+        copy = remote(
+            all_mixed.at[core, source],
+            all_mixed.at[core, source],
+            forward_sems,
+            source,
+            me_ctx,
+            z * 2 + 1 - core,
+        )
+        copy.start()
+        forward_copies.append(copy)
 
     def feature_gradient(tile, carry):
         cols = column(tile)
@@ -598,28 +623,6 @@
         return carry
 
     lax.fori_loop(0, chans // TILE, feature_gradient, 0)
-
-    forward_copies = []
-    for source in range(n_ctx):
-        @pl.when(me_ctx == source)
-        def _():
-            own_relay.wait()
-
-        @pl.when(me_ctx != source)
-        def _(source=source):
-            slot = all_mixed.at[core, source]
-            remote(line_mixed.at[0], slot, relay_sems, source, me_ctx, me_ch).wait_recv()
-
-        copy = remote(
-            all_mixed.at[core, source],
-            all_mixed.at[core, source],
-            forward_sems,
-            source,
-            me_ctx,
-            z * 2 + 1 - core,
-        )
-        copy.start()
-        forward_copies.append(copy)
 
     arrived(lag_copies)
 
@@ -743,7 +746,6 @@
         staged,
         staged,
         blocks,
-        pltpu.VMEM((block_len, chans), F32),
         pltpu.VMEM((3, block_len + NEXT_EDGE, chans), F32),
         pltpu.VMEM((3, NEXT_EDGE, chans), F32),
         pltpu.VMEM((n_ctx, 3, taps + 1, chans), F32),
@@ -801,7 +803,7 @@
             in_place,
         ],
         scratch_shapes=[pltpu.SemaphoreType.DMA((3,))],
-        compiler_params=pltpu.CompilerParams(vmem_limit_bytes=32 * 1024 * 1024),
+        compiler_params=pltpu.CompilerParams(vmem_limit_bytes=60 * 1024 * 1024),
         cost_estimate=pl.CostEstimate(
             flops=4 * 10**9, bytes_accessed=12 * 2**20, transcendentals=0
         ),

time: 107 us -> 135 us (1.26)
  Pallas kernels: 99.8 us -> 135 us
  local copies, waits for them, and re-layouts: 5.87 us -> 0 us
    pallas_call x1, Pallas kernels: 6.45 us -> 46.1 us  [fused(): pl.pallas_call(product_kernel, grid=(2 * per_half,), out_shape=[jax.Shape...]
    unnamed x10 -> x0, local copies, waits for them, and re-layouts: 5.87 us -> none
    pallas_call x1, Pallas kernels: 93.3 us -> 88.4 us  [fused(): pl.pallas_call(fused_kernel, out_shape=[jax.ShapeDtypeStruct(features.sha...]
where the time goes in v4:
time: 135 us
  Pallas kernels  135 us (100%)
    pallas_call x1, Pallas kernels, fused(): pl.pallas_call(fused_kernel, out_shape=[jax.ShapeDtypeStruct(features.sha...  88.4 us
    pallas_call x1, Pallas kernels, fused(): pl.pallas_call(product_kernel, grid=(2 * per_half,), out_shape=[jax.Shape...  46.1 us

profile of v4, /device:TPU:7, one launch (start us, length us, event | category | flops | bytes accessed | tf_op | source)
XLA Modules:
  0.0 135.2 jit_solution(2319186083558626516)
XLA Ops:
  0.6 88.4 %shard_map.120 = (bf16[3,128,1024]{2,1,0:T(8,128)(2,1)}, f32[3,7,1024]{2,1,0:T(8,128)}, f32[128,1024]{1,0:T(8,128)}, bf16[4,128,1024]{2,1,0:T(8,128)(2,1)}, bf16[2,4,128,1024]{3,2,1,0:T(8,128)(2,1)}) custom-call(bf16[3,128,1024]{2,1,0:T(8,128)(2,1)} %features.1, f32[3,7,1024]{2,1,0:T(8,128)} %short_kernel.1, bf16[128,1024]{1,0:T(8,128)(2,1)} %long_filter.1, ...), custom_call_target="tpu_custom_call" | custom-call | flops 8000000000 | bytes 29360128 | tf_op jit(solution)/shard_map/pallas_call | solution.py:763
  89.0 46.1 %shard_map.121 = (f32[2048,1024]{1,0:T(8,128)}, bf16[3,128,1024]{2,1,0:T(8,128)(2,1)}, f32[3,7,1024]{2,1,0:T(8,128)}, f32[128,1024]{1,0:T(8,128)}) custom-call(bf16[2,512,1024]{2,1,0:T(8,128)(2,1)} %bitcast.2, bf16[512,1024]{1,0:T(8,128)(2,1)} %bitcast.3, bf16[3,128,1024]{2,1,0:T(8,128)(2,1)} %get-tuple-element.15.features_from, ...), custom_call_target="tpu_custom_call" | custom-call | flops 4000000000 | bytes 12582912 | tf_op jit(solution)/shard_map/pallas_call | solution.py:783

commit v5 on v4

--- a/solution.py
+++ b/solution.py
@@ -679,19 +679,36 @@
     features_to,
     kernel_to,
     filter_to,
+    features_held,
+    kernel_held,
+    filter_held,
     sems,
 ):
     step, steps = pl.program_id(0), pl.num_programs(0)
-    pairs = [(features_from, features_to), (kernel_from, kernel_to), (filter_from, filter_to)]
-    copies = [
-        pltpu.make_async_copy(source, target, sems.at[index])
-        for index, (source, target) in enumerate(pairs)
+    ways = [
+        (features_from, features_held, features_to),
+        (kernel_from, kernel_held, kernel_to),
+        (filter_from, filter_held, filter_to),
+    ]
+    takes = [
+        pltpu.make_async_copy(source, held, sems.at[0, index])
+        for index, (source, held, _) in enumerate(ways)
+    ]
+    gives = [
+        pltpu.make_async_copy(held, target, sems.at[1, index])
+        for index, (_, held, target) in enumerate(ways)
     ]
 
     @pl.when(step == 0)
     def _():
-        for copy in copies:
+        for copy in takes:
             copy.start()
+
+    @pl.when(step == steps // 2)
+    def _():
+        for take, give in zip(takes, gives):
+            take.wait()
+            give.start()
 
     grad_weight[...] = lax.dot_general(
         mixed_tile[0],
@@ -702,7 +719,7 @@
 
     @pl.when(step == steps - 1)
     def _():
-        for copy in copies:
+        for copy in gives:
             copy.wait()
 
 
@@ -770,7 +787,7 @@
             jax.ShapeDtypeStruct((2, n_ctx, block_len, chans), BF16),
         ],
         in_specs=[in_vmem, in_vmem, in_vmem, in_place] + [in_vmem] * 5,
-        out_specs=[in_vmem, in_vmem, in_vmem, in_place, in_place],
+        out_specs=[in_vmem] * 5,
         scratch_shapes=scratch,
         compiler_params=pltpu.CompilerParams(
             collective_id=0, has_side_effects=True, vmem_limit_bytes=56 * 1024 * 1024
@@ -802,7 +819,12 @@
             in_place,
             in_place,
         ],
-        scratch_shapes=[pltpu.SemaphoreType.DMA((3,))],
+        scratch_shapes=[
+            pltpu.VMEM(grad_features.shape, BF16),
+            pltpu.VMEM(grad_kernel.shape, F32),
+            pltpu.VMEM(grad_filter.shape, F32),
+            pltpu.SemaphoreType.DMA((2, 3)),
+        ],
         compiler_params=pltpu.CompilerParams(vmem_limit_bytes=60 * 1024 * 1024),
         cost_estimate=pl.CostEstimate(
             flops=4 * 10**9, bytes_accessed=12 * 2**20, transcendentals=0

time: 135 us -> 98.6 us (0.73)
  Pallas kernels: 135 us -> 97.6 us
    pallas_call x1, Pallas kernels: 46.1 us -> 8.82 us  [fused(): pl.pallas_call(product_kernel, grid=(2 * per_half,), out_shape=[jax.Shape...]
where the time goes in v5:
time: 98.6 us; the launch traced here: 98.3 us
  Pallas kernels  97.6 us (99%)
    pallas_call x1, Pallas kernels, fused(): pl.pallas_call(fused_kernel, out_shape=[jax.ShapeDtypeStruct(features.sha...  88.8 us
    pallas_call x1, Pallas kernels, fused(): pl.pallas_call(product_kernel, grid=(2 * per_half,), out_shape=[jax.Shape...  8.82 us

profile of v5, /device:TPU:7, one launch (start us, length us, event | category | flops | bytes accessed | tf_op | source)
XLA Modules:
  0.0 98.3 jit_solution(18406706878521789680)
XLA Ops:
  0.6 88.8 %shard_map.120 = (bf16[3,128,1024]{2,1,0:T(8,128)(2,1)}, f32[3,7,1024]{2,1,0:T(8,128)}, f32[128,1024]{1,0:T(8,128)}, bf16[4,128,1024]{2,1,0:T(8,128)(2,1)}, bf16[2,4,128,1024]{3,2,1,0:T(8,128)(2,1)}) custom-call(bf16[3,128,1024]{2,1,0:T(8,128)(2,1)} %features.1, f32[3,7,1024]{2,1,0:T(8,128)} %short_kernel.1, bf16[128,1024]{1,0:T(8,128)(2,1)} %long_filter.1, ...), custom_call_target="tpu_custom_call" | custom-call | flops 8000000000 | bytes 29360128 | tf_op jit(solution)/shard_map/pallas_call | solution.py:780
  89.5 8.8 %shard_map.121 = (f32[2048,1024]{1,0:T(8,128)}, bf16[3,128,1024]{2,1,0:T(8,128)(2,1)}, f32[3,7,1024]{2,1,0:T(8,128)}, f32[128,1024]{1,0:T(8,128)}) custom-call(bf16[2,512,1024]{2,1,0:T(8,128)(2,1)} %bitcast.2, bf16[512,1024]{1,0:T(8,128)(2,1)} %bitcast.3, bf16[3,128,1024]{2,1,0:T(8,128)(2,1)} %get-tuple-element.15.features_from, ...), custom_call_target="tpu_custom_call" | custom-call | flops 4000000000 | bytes 12582912 | tf_op jit(solution)/shard_map/pallas_call | solution.py:800
